TPU v7x, 512 devices: a whole 4x8x8 slice. The times are simulated.
512 devices in a mesh: grp: 16 (over z, core), pt: 32 (over x, y).
Axes of the slice: x: 4, y: 8, z: 8, core: 2. Of those that a mesh axis runs over, the one named last changes fastest.
Arguments:
- features: bfloat16 [262144, 512], P(('grp', 'pt')), as said below
- cotangent: bfloat16 [262144, 512], P(('grp', 'pt')), may hold values from -6 to 6
- conv_weight: float32 [27, 512], replicated, may hold values from -1.5 to 1.5
- neighbours: int32 [262144, 27], P(('grp', 'pt')), may hold values from -1 to 639, as said below
- halo_index: int32 [512, 128], P(('grp', 'pt')), may hold values from 0 to 511, as said below
- send_index: int32 [512, 32, 32], P(('grp', 'pt')), may hold values from -1 to 511, as said below
- curve_slot: int32 [262144], P(('grp', 'pt')), may hold values from 0 to 1023, as said below
Outputs:
- grad_features: bfloat16 [262144, 512], P(('grp', 'pt'))
- grad_conv: float32 [27, 512], replicated
Inputs may be any that keep to these rules, and one draw needn't show every extreme that they name: `features`: each feature lies within -10 to 10. `neighbours`: offset 27 // 2 names the point itself; other entries name own rows, borrowed rows (512 and up) or -1. `halo_index`: the 64 rows of each half are distinct. `send_index`: for every tile and curve shard the used slots come first and the rest hold -1; a tile sends each of its rows exactly once; every tile fills all 32 slots for one curve shard, and every curve shard receives 512 rows. `curve_slot`: within each curve shard every used slot appears once.
All inputs are finite; a program needn't handle non-finite values.
Results may differ from a plain program's by a relative error of at most 0.0045.
The roundings to bfloat16 on the way count: a program that leaves them out, or rounds other values in their place, can miss the bound.
Values may be sent and summed in bfloat16 or wider, within the bound.
A program may use at most 64 MiB of HBM per device.

v0:
```python
import jax
import jax.numpy as jnp
from jax import lax
from jax.sharding import PartitionSpec as P

D = 512
HEADS = 32
PATCH = 512


def padded_2(cells, sides, width):
    for axis, dim in sides:
        count = lax.axis_size(axis)
        ends = count - 1
        head = lax.slice_in_dim(cells, 0, width, axis=dim)
        tail = lax.slice_in_dim(cells, cells.shape[dim] - width, cells.shape[dim], axis=dim)
        cells = jnp.concatenate(
            [
                lax.ppermute(tail, axis, [(i, (i + 1) % count) for i in range(ends)]),
                cells,
                lax.ppermute(head, axis, [((i + 1) % count, i) for i in range(ends)]),
            ],
            axis=dim,
        )
    return cells


def conv_forward(padded, tap_index, conv_weight):
    row_count = tap_index.shape[0]

    def add_tap(kernel_tap, accum):
        picked = padded[tap_index[:, kernel_tap]].astype(jnp.float32)
        return accum + conv_weight[kernel_tap] * picked

    start_value = jnp.zeros((row_count, padded.shape[1]), jnp.float32)
    summed = lax.fori_loop(0, conv_weight.shape[0], add_tap, start_value)
    return (padded[:row_count].astype(jnp.float32) + summed).astype(jnp.bfloat16)


def conv_backward(padded, tap_index, grad_rows, conv_weight):
    grad_float = grad_rows.astype(jnp.float32)

    def add_tap(kernel_tap, carry):
        spread, terms = carry
        picked = tap_index[:, kernel_tap]
        spread = spread.at[picked].add(conv_weight[kernel_tap] * grad_float)
        terms = terms.at[kernel_tap].set(
            jnp.sum(grad_float * padded[picked].astype(jnp.float32), axis=0)
        )
        return (spread, terms)

    start_value = (jnp.zeros(padded.shape, jnp.float32), jnp.zeros(conv_weight.shape, jnp.float32))
    return lax.fori_loop(0, conv_weight.shape[0], add_tap, start_value)


def pair_grad(queries, upstream, head_dim):
    scale = head_dim ** (-0.5)
    scores = (
        jnp.einsum("qhd,khd->hqk", queries, queries, preferred_element_type=jnp.float32) * scale
    )
    probs = jax.nn.softmax(scores, axis=-1)
    probs_low = probs.astype(jnp.bfloat16)
    dvalue = jnp.einsum("hqk,qhd->khd", probs_low, upstream, preferred_element_type=jnp.float32)
    dprobs = jnp.einsum("qhd,khd->hqk", upstream, queries, preferred_element_type=jnp.float32)
    delta = jnp.sum(probs * dprobs, axis=-1, keepdims=True)
    dscores = (probs * (dprobs - delta)).astype(jnp.bfloat16)
    dquery = (
        jnp.einsum("hqk,khd->qhd", dscores, queries, preferred_element_type=jnp.float32) * scale
    )
    dkey = jnp.einsum("hqk,qhd->khd", dscores, queries, preferred_element_type=jnp.float32) * scale
    return dquery + dkey + dvalue


def attention_grad(curve_cols, cot_cols):
    row_count, col_count = curve_cols.shape
    head_dim = D // HEADS
    pair_count = col_count // (2 * head_dim)
    patch_count = row_count // PATCH

    def to_blocks(values):
        shaped = values.reshape(patch_count, PATCH, pair_count, 2, head_dim)
        return shaped.transpose(0, 2, 1, 3, 4).reshape(patch_count * pair_count, PATCH, 2, head_dim)

    grads = lax.map(
        lambda pair_in: pair_grad(pair_in[0], pair_in[1], head_dim),
        (to_blocks(curve_cols), to_blocks(cot_cols)),
    )
    grads = grads.reshape(patch_count, pair_count, PATCH, 2, head_dim).transpose(0, 2, 1, 3, 4)
    grads = grads.reshape(row_count, col_count)
    return (cot_cols.astype(jnp.float32) + grads).astype(jnp.bfloat16)


def on_device(features, cotangent, conv_weight, neighbours, halo_index, send_index, curve_slot):
    row_count, width = features.shape
    rim_rows = halo_index.shape[1] // 2
    peer_count = send_index.shape[1]
    slot_count = send_index.shape[2]
    lent_rows = halo_index[0]
    lent = features[lent_rows]
    bordered = padded_2(lent, (("grp", 0),), rim_rows)
    padded = jnp.concatenate(
        [
            features,
            bordered[:rim_rows],
            bordered[3 * rim_rows :],
            jnp.zeros((1, width), jnp.bfloat16),
        ],
        axis=0,
    )
    tap_index = jnp.where(neighbours < 0, row_count + 2 * rim_rows, neighbours)
    hidden = conv_forward(padded, tap_index, conv_weight)
    targets = send_index[0]
    outgoing = jnp.where(
        (targets >= 0)[..., None], hidden[jnp.maximum(targets, 0)], jnp.zeros((), jnp.bfloat16)
    )
    incoming = lax.all_to_all(outgoing, "pt", split_axis=0, concat_axis=0, tiled=True)
    curve = incoming.reshape(peer_count * slot_count, width)[curve_slot]
    positions = (
        jnp.full((peer_count * slot_count,), -1, jnp.int32)
        .at[curve_slot]
        .set(jnp.arange(row_count, dtype=jnp.int32))
    )
    flat_targets = targets.reshape(-1)
    slot_ids = jnp.arange(peer_count * slot_count, dtype=jnp.int32)
    tile_slot = (
        jnp.zeros((row_count + 1,), jnp.int32)
        .at[jnp.where(flat_targets >= 0, flat_targets, row_count)]
        .set(slot_ids)[:row_count]
    )
    all_heads = attention_grad(curve, cotangent)
    gathered = all_heads[jnp.maximum(positions, 0)]
    filled = jnp.where((positions >= 0)[:, None], gathered, jnp.zeros((), jnp.bfloat16))
    returned = lax.all_to_all(
        filled.reshape(peer_count, slot_count, all_heads.shape[1]),
        "pt",
        split_axis=0,
        concat_axis=0,
        tiled=True,
    )
    grad_hidden = returned.reshape(peer_count * slot_count, width)[tile_slot]
    spread, terms = conv_backward(padded, tap_index, grad_hidden, conv_weight)
    echoed = padded_2(
        spread[row_count : row_count + 2 * rim_rows].astype(jnp.bfloat16), (("grp", 0),), rim_rows
    ).astype(jnp.float32)
    grad_total = grad_hidden.astype(jnp.float32) + spread[:row_count]
    grad_total = grad_total.at[lent_rows[:rim_rows]].add(echoed[:rim_rows])
    grad_total = grad_total.at[lent_rows[rim_rows:]].add(echoed[3 * rim_rows :])
    grad_conv = lax.psum(terms, ("grp", "pt"))
    return (grad_total.astype(jnp.bfloat16), grad_conv)


def solution(mesh):
    in_specs = (
        P(("grp", "pt"), None),
        P(("grp", "pt"), None),
        P(),
        P(("grp", "pt"), None),
        P(("grp", "pt"), None),
        P(("grp", "pt"), None, None),
        P(("grp", "pt")),
    )
    out_specs = (P(("grp", "pt"), None), P())
    return jax.shard_map(
        on_device, mesh=mesh, in_specs=in_specs, out_specs=out_specs, check_vma=False
    )
```

profile of v0, /device:TPU:1, one launch (start us, length us, event | category | flops | bytes accessed | tf_op | source)
XLA Modules:
  0.0 716.1 jit_solution(10902012644308180097)
XLA Ops:
  17.1 86.9 %while.42 = (s32[]{:T(128)}, f32[512,512]{1,0:T(8,128)S(1)}, f32[27,512]{1,0:T(8,128)}, s32[512,27]{0,1:T(8,128)S(1)}, bf16[641,512]{1,0:T(8,128)(2,1)S(1)}, /*index=5*/s32[]{:T(128)}, s32[]{:T(128)}) while((s32[]{:T(128)}, f32[512,512]{1,0:T(8,128)S(1)}, f32[27,512]{1,0:T(8,128)}, s32[512,27]{0,1:T(8,128)S(1)}, ...), condition=%wide.region_2.3_spmd.clone, body=%wide.region_1.2_spmd.clone.sunk | while | flops 1051139 | bytes 3688543 | solution.py:36
  109.4 8.3 %all-to-all-start = ((bf16[32,32,512]{2,1,0:T(8,128)(2,1)}), bf16[32,32,512]{2,1,0:T(8,128)(2,1)S(1)}, u32[]{:S(2)}, u32[]{:S(2)}) async-start(bf16[32,32,512]{2,1,0:T(8,128)(2,1)} %broadcast_select_fusion.1), calls=%async_computation | async-start | bytes 2097152 | tf_op jit(solution)/shard_map/all_to_all | solution.py:116
  121.3 23.8 %all-to-all-done = bf16[32,32,512]{2,1,0:T(8,128)(2,1)S(1)} async-done(((bf16[32,32,512]{2,1,0:T(8,128)(2,1)}), bf16[32,32,512]{2,1,0:T(8,128)(2,1)S(1)}, u32[]{:S(2)}, u32[]{:S(2)}) %all-to-all-start) | async-done | bytes 1048608 | tf_op jit(solution)/shard_map/all_to_all | solution.py:116
  148.0 132.4 %while.40 = (s32[]{:T(128)}, f32[16,512,2,16]{1,3,2,0:T(8,128)}, bf16[16,512,2,16]{1,3,2,0:T(8,128)(2,1)}, bf16[16,512,2,16]{1,3,2,0:T(8,128)(2,1)}, s32[]{:T(128)}) while((s32[]{:T(128)}, f32[16,512,2,16]{1,3,2,0:T(8,128)}, bf16[16,512,2,16]{1,3,2,0:T(8,128)(2,1)}, bf16[16,512,2,16]{1,3,2,0:T(8,128)(2,1)}, s32[]{:T(128)}) %tuple.103), condition=%wide.region_7.8_spmd, body=%wide.region_3.0_spmd.sunk | while | flops 108053504 | bytes 14217277 | solution.py:84
  296.7 21.2 %all-to-all-done.1 = bf16[32,32,512]{2,1,0:T(8,128)(2,1)S(1)} async-done(((bf16[32,32,512]{2,1,0:T(8,128)(2,1)}), bf16[32,32,512]{2,1,0:T(8,128)(2,1)S(1)}, u32[]{:S(2)}, u32[]{:S(2)}) %all-to-all-start.1) | async-done | bytes 1048608 | tf_op jit(solution)/shard_map/all_to_all | solution.py:133
  321.3 279.1 %while.41 = (s32[]{:T(128)}, f32[641,512]{1,0:T(8,128)}, f32[27,512]{1,0:T(8,128)S(1)}, s32[512,27]{0,1:T(8,128)S(1)}, f32[27,512]{1,0:T(8,128)}, /*index=5*/f32...) while((s32[]{:T(128)}, f32[641,512]{1,0:T(8,128)}, ...), condition=%wide.region_13.14_spmd, body=%wide.region_9.13_spmd.sunk | while | flops 1313291 | bytes 5013643 | solution.py:53
  325.6 6.0 scatter_custom_fusion.13
  336.0 6.0 scatter_custom_fusion.13
  346.3 6.0 scatter_custom_fusion.13
  367.0 6.0 scatter_custom_fusion.13
  377.3 6.0 scatter_custom_fusion.13
  387.6 6.0 scatter_custom_fusion.13
  398.0 6.0 scatter_custom_fusion.13
  408.3 6.0 scatter_custom_fusion.13
  418.7 6.0 scatter_custom_fusion.13
  429.0 6.0 scatter_custom_fusion.13
  439.3 6.0 scatter_custom_fusion.13
  449.7 6.0 scatter_custom_fusion.13
  460.0 6.0 scatter_custom_fusion.13
  470.3 6.0 scatter_custom_fusion.13
  501.3 6.0 scatter_custom_fusion.13
  511.7 6.0 scatter_custom_fusion.13
  522.0 6.0 scatter_custom_fusion.13
  532.4 6.0 scatter_custom_fusion.13
  542.7 6.0 scatter_custom_fusion.13
  553.0 6.0 scatter_custom_fusion.13
  563.4 6.0 scatter_custom_fusion.13
  573.7 6.0 scatter_custom_fusion.13
  584.0 6.0 scatter_custom_fusion.13
  594.4 6.0 scatter_custom_fusion.13
  602.0 8.5 %collective-permute-start.2 = (bf16[64,512]{1,0:T(8,128)(2,1)S(1)}, bf16[64,512]{1,0:T(8,128)(2,1)S(1)}, u32[]{:S(2)}, u32[]{:S(2)}) collective-permute-start(bf16[64,512]{1,0:T(8,128)(2,1)S(1)} %get-tuple-element.325), channel_id=1, source_target_pairs={{0,32},{32,64},{64,96},{96,128},{128,160},{160,192},{192,224},{224... | collective-permute-start | bytes 196616 | tf_op jit(solution)/shard_map/ppermute | solution.py:19
  612.5 99.9 %psum.7 = f32[27,512]{1,0:T(8,128)} all-reduce(f32[27,512]{1,0:T(8,128)S(1)} %get-tuple-element.268), channel_id=1, replica_groups=mesh['grp'=16,'pt'=32] {'grp','pt'}, use_global_device_ids=true, to_apply=%region_16.17 | all-reduce | flops 13824 | bytes 110592 | tf_op jit(solution)/shard_map/psum | solution.py:148
  (493 shorter events, 407.0 us)
Async XLA Ops:
  3.3 12.5 %collective-permute-start = (bf16[64,512]{1,0:T(8,128)(2,1)S(1)}, bf16[64,512]{1,0:T(8,128)(2,1)S(1)}, u32[]{:S(2)}, u32[]{:S(2)}) collective-permute-start(bf16[64,512]{1,0:T(8,128)(2,1)S(1)} %get-tuple-element.327), channel_id=1, source_target_pairs={{0,32},{32,64},{64,96},{96,128},{128,160},{160,192},{192,224},{224... | collective-permute-start | bytes 196616 | tf_op jit(solution)/shard_map/ppermute | solution.py:19
  8.7 7.1 collective-permute-start.1
  17.1 86.9 %copy-start.1 = (bf16[512,512]{1,0:T(8,128)(2,1)S(1)}, bf16[512,512]{1,0:T(8,128)(2,1)}, u32[]{:S(2)}) copy-start(bf16[512,512]{1,0:T(8,128)(2,1)} %param.15) | copy-start | bytes 1572868
  108.1 9.6 %copy-start.2 = (bf16[512,512]{1,0:T(8,128)(2,1)S(1)}, bf16[512,512]{1,0:T(8,128)(2,1)}, u32[]{:S(2)}) copy-start(bf16[512,512]{1,0:T(8,128)(2,1)} %param.16) | copy-start | bytes 1572868
  109.4 9.3 %copy-start.5 = (s32[512]{0:T(512)S(1)}, s32[512]{0:T(512)}, u32[]{:S(2)}) copy-start(s32[512]{0:T(512)} %param.21) | copy-start | bytes 6148
  109.4 35.7 %all-to-all-start = ((bf16[32,32,512]{2,1,0:T(8,128)(2,1)}), bf16[32,32,512]{2,1,0:T(8,128)(2,1)S(1)}, u32[]{:S(2)}, u32[]{:S(2)}) async-start(bf16[32,32,512]{2,1,0:T(8,128)(2,1)} %broadcast_select_fusion.1), calls=%async_computation | async-start | bytes 2097152 | tf_op jit(solution)/shard_map/all_to_all | solution.py:116
  286.1 5.9 copy-start.3
  286.1 10.5 %copy-start.6 = (s32[1,128]{1,0:T(1,128)S(1)}, s32[1,128]{1,0:T(1,128)}, u32[]{:S(2)}) copy-start(s32[1,128]{1,0:T(1,128)} %param.19) | copy-start | bytes 1540
  287.4 30.6 %all-to-all-start.1 = ((bf16[32,32,512]{2,1,0:T(8,128)(2,1)}), bf16[32,32,512]{2,1,0:T(8,128)(2,1)S(1)}, u32[]{:S(2)}, u32[]{:S(2)}) async-start(bf16[32,32,512]{2,1,0:T(8,128)(2,1)} %broadcast_select_fusion.2), calls=%async_computation.1 | async-start | bytes 2097152 | tf_op jit(solution)/shard_map/all_to_all | solution.py:133
  319.9 1.4 copy-start.4
  600.4 11.9 %copy-start = (f32[641,512]{1,0:T(8,128)S(1)}, f32[641,512]{1,0:T(8,128)}, u32[]{:S(2)}) copy-start(f32[641,512]{1,0:T(8,128)} %get-tuple-element.267) | copy-start | bytes 3938308
  602.0 110.5 %collective-permute-start.2 = (bf16[64,512]{1,0:T(8,128)(2,1)S(1)}, bf16[64,512]{1,0:T(8,128)(2,1)S(1)}, u32[]{:S(2)}, u32[]{:S(2)}) collective-permute-start(bf16[64,512]{1,0:T(8,128)(2,1)S(1)} %get-tuple-element.325), channel_id=1, source_target_pairs={{0,32},{32,64},{64,96},{96,128},{128,160},{160,192},{192,224},{224... | collective-permute-start | bytes 196616 | tf_op jit(solution)/shard_map/ppermute | solution.py:19
  610.4 102.0 %collective-permute-start.3 = (bf16[64,512]{1,0:T(8,128)(2,1)S(1)}, bf16[64,512]{1,0:T(8,128)(2,1)S(1)}, u32[]{:S(2)}, u32[]{:S(2)}) collective-permute-start(bf16[64,512]{1,0:T(8,128)(2,1)S(1)} %get-tuple-element.326), channel_id=1, source_target_pairs={{32,0},{64,32},{96,64},{128,96},{160,128},{192,160},{224,192},{256... | collective-permute-start | bytes 196616 | tf_op jit(solution)/shard_map/ppermute | solution.py:21
where the time goes:
time: 727 us; the launch traced here: 716 us
  other arithmetic  258 us (35%)
  local copies, waits for them, and re-layouts  153 us (21%)
  matrix products  123 us (17%)
  blocking collectives  99.9 us (14%)
  waiting for transfers between devices  45 us (6%)
  starting transfers between devices  33.4 us (5%)
    scatter-add x27, other arithmetic, add_tap(): spread = spread.at[picked].add(conv_weight[kernel_tap] * grad_float)  162 us
    psum x1, blocking collectives, on_device(): grad_conv = lax.psum(terms, ('grp', 'pt'))  99.9 us
    another operation x55, other arithmetic  57.7 us
    gather x27, local copies, waits for them, and re-layouts, add_tap(): picked = padded[tap_index[:, kernel_tap]].astype(jnp.float32)  53.2 us
    gather x27, local copies, waits for them, and re-layouts, add_tap(): padded[picked].astype(jnp.float32)  53.2 us
    dot_general x16, matrix products, pair_grad(): jnp.einsum('hqk,qhd->khd', probs_low, upstream, preferred_element_type=jn...  41.4 us
    sub x16, matrix products, pair_grad(): probs = jax.nn.softmax(scores, axis=-1)  27.2 us
    all_to_all x1, waiting for transfers between devices, on_device(): lax.all_to_all(outgoing, 'pt', split_axis=0, concat_axis=0, tiled=True)  23.8 us
  transfers between devices with their start and end apart: 6, of which 2 were waited for; matrix products, arithmetic and copies ran while one was open for 2% of the time, Pallas kernels for 0%

commit v1 on v0

v1 whole, which is shorter than its diff:
```python
import functools

import jax
import jax.numpy as jnp
from jax import lax
from jax.experimental import pallas as pl
from jax.experimental.pallas import tpu as pltpu
from jax.sharding import PartitionSpec as P

D = 512
ROWS = 512
RIM = 64
TABLE = ROWS + 2 * RIM
TAPS = 27
CENTRE = TAPS // 2
HEAD_DIM = 16
LANES = 128
BF16 = jnp.bfloat16
F32 = jnp.float32
I16 = jnp.int16
VMEM = pl.BlockSpec(memory_space=pltpu.VMEM)
MESH = pl.DeviceIdType.MESH


def dot(a, b, dims=((1,), (0,))):
    return lax.dot_general(a, b, (dims, ((), ())), preferred_element_type=F32)


def pick(mask):
    return jnp.where(mask, jnp.ones((), BF16), jnp.zeros((), BF16))


def rows_of(index_row, width):
    count = index_row.shape[1]
    column = jnp.broadcast_to(index_row, (LANES, count)).T.astype(I16)
    lane = lax.broadcasted_iota(jnp.int32, (count, LANES), 1).astype(I16)
    blocks = [pick(column == lane + jnp.asarray(start, I16)) for start in range(0, width, LANES)]
    return jnp.concatenate(blocks, axis=1)


def columns_of(index_row, height):
    count = index_row.shape[1]
    row = jnp.broadcast_to(index_row, (16, count)).astype(I16)
    sub = lax.broadcasted_iota(jnp.int32, (16, count), 0).astype(I16)
    blocks = [pick(row == sub + jnp.asarray(start, I16)) for start in range(0, height, 16)]
    return jnp.concatenate(blocks, axis=0)


def lend_kernel(halo_ref, features_ref, lent_ref):
    lent_ref[...] = dot(rows_of(halo_ref[...], ROWS), features_ref[...]).astype(BF16)


def other_tap(step):
    return jnp.where(step < CENTRE, step, step + 1)


def forward_kernel(taps_ref, weight_ref, send_ref, padded_ref, out_ref, acc_ref):
    own = padded_ref[:ROWS, :].astype(F32)
    acc_ref[...] = own + own * weight_ref[CENTRE : CENTRE + 1, :]

    def tap(step, _):
        k = other_tap(step)
        picked = dot(rows_of(taps_ref[pl.ds(k, 1), :], TABLE), padded_ref[...])
        acc_ref[...] += picked * weight_ref[pl.ds(k, 1), :]
        return 0

    lax.fori_loop(0, TAPS - 1, tap, 0)
    hidden = acc_ref[...].astype(BF16)
    out_ref[...] = dot(rows_of(send_ref[...], ROWS), hidden).astype(BF16)


def attention_kernel(curve_ref, cotangent_ref, slots_ref, out_ref, rows_ref, grad_ref):
    rows_ref[...] = dot(rows_of(curve_ref[...], slots_ref.shape[0]), slots_ref[...]).astype(BF16)

    def group(g, _):
        span = pl.ds(pl.multiple_of(g * LANES, LANES), LANES)
        rows = rows_ref[:, span]
        cot = cotangent_ref[:, span]
        scaled = rows * jnp.asarray(HEAD_DIM**-0.5, BF16)
        head_of = lax.broadcasted_iota(jnp.int32, (ROWS, LANES), 1) // HEAD_DIM
        total = cot.astype(F32)
        for h in range(LANES // HEAD_DIM):
            inside = head_of == h
            keys = jnp.where(inside, rows, jnp.zeros((), BF16))
            scores = dot(keys, scaled, ((1,), (1,)))
            dprobs = dot(keys, cot, ((1,), (1,)))
            weights = jnp.exp(scores - jnp.max(scores, axis=0, keepdims=True))
            probs = weights * (1.0 / jnp.sum(weights, axis=0, keepdims=True))
            delta = jnp.sum(probs * dprobs, axis=0, keepdims=True)
            dscores = (probs * (dprobs - delta)).astype(BF16)
            grads = dot(probs.astype(BF16), cot) + dot(dscores, scaled)
            grads = grads + dot(dscores, scaled, ((0,), (0,)))
            total = total + jnp.where(inside, grads, 0.0)
        grad_ref[:, span] = total.astype(BF16)
        return 0

    lax.fori_loop(0, D // LANES, group, 0)
    out_ref[...] = dot(columns_of(curve_ref[...], slots_ref.shape[0]), grad_ref[...]).astype(BF16)


def backward_kernel(
    taps_ref, weight_ref, send_ref, padded_ref, slots_ref, total_ref, rim_ref, terms_ref, grad_ref, spread_ref
):
    grad_ref[...] = dot(columns_of(send_ref[...], ROWS), slots_ref[...]).astype(BF16)
    grad = grad_ref[...].astype(F32)
    spread_ref[:ROWS, :] = grad + grad * weight_ref[CENTRE : CENTRE + 1, :]
    spread_ref[ROWS:, :] = jnp.zeros((2 * RIM, D), F32)
    terms_ref[CENTRE] = jnp.sum(grad * padded_ref[:ROWS, :].astype(F32), axis=0, keepdims=True)

    def tap(step, _):
        k = other_tap(step)
        landed = dot(columns_of(taps_ref[pl.ds(k, 1), :], TABLE), grad_ref[...])
        spread_ref[...] += landed * weight_ref[pl.ds(k, 1), :]
        terms_ref[k] = jnp.sum(landed * padded_ref[...].astype(F32), axis=0, keepdims=True)
        return 0

    lax.fori_loop(0, TAPS - 1, tap, 0)
    total_ref[...] = spread_ref[:ROWS, :]
    rim_ref[...] = spread_ref[ROWS:, :].astype(BF16)


def finish_kernel(halo_ref, total_ref, echoed_ref, out_ref):
    landed = dot(columns_of(halo_ref[...], ROWS), echoed_ref[...])
    out_ref[...] = (total_ref[...] + landed).astype(BF16)


def reduce_kernel(
    regions, peers, terms_ref, out_ref, parts, part, sums, whole, send_sem, part_sem, sum_sem, whole_sem
):
    grp = lax.axis_index("grp")
    me = lax.axis_index("pt")
    barrier = pltpu.get_barrier_semaphore()

    def greet_peer(step, _):
        peer = (me + step) % peers
        pl.semaphore_signal(barrier, inc=1, device_id=(grp, peer), device_id_type=MESH)
        return 0

    def greet_region(step, _):
        other = (grp + step) % regions
        pl.semaphore_signal(barrier, inc=1, device_id=(other, me), device_id_type=MESH)
        return 0

    lax.fori_loop(1, peers, greet_peer, 0)
    lax.fori_loop(1, regions, greet_region, 0)
    pl.semaphore_wait(barrier, peers - 1 + regions - 1)

    def to_owner(step):
        peer = (me + step) % peers
        return peer, pltpu.make_async_remote_copy(
            src_ref=terms_ref.at[peer % TAPS],
            dst_ref=parts.at[me],
            send_sem=send_sem.at[peer],
            recv_sem=part_sem.at[me],
            device_id=(grp, peer),
            device_id_type=MESH,
        )

    def from_peer(step):
        peer = (me + peers - step) % peers
        return pltpu.make_async_remote_copy(
            src_ref=terms_ref.at[0],
            dst_ref=parts.at[peer],
            send_sem=send_sem.at[peer],
            recv_sem=part_sem.at[peer],
            device_id=(grp, peer),
            device_id_type=MESH,
        )

    def to_region(step):
        other = (grp + step) % regions
        return pltpu.make_async_remote_copy(
            src_ref=part,
            dst_ref=sums.at[grp],
            send_sem=send_sem.at[peers + other],
            recv_sem=sum_sem.at[grp],
            device_id=(other, me),
            device_id_type=MESH,
        )

    def from_region(step):
        other = (grp + regions - step) % regions
        return pltpu.make_async_remote_copy(
            src_ref=part,
            dst_ref=sums.at[other],
            send_sem=send_sem.at[peers + other],
            recv_sem=sum_sem.at[other],
            device_id=(other, me),
            device_id_type=MESH,
        )

    def to_all(step):
        peer = (me + step) % peers
        return pltpu.make_async_remote_copy(
            src_ref=whole.at[me],
            dst_ref=whole.at[me],
            send_sem=send_sem.at[peers + regions + peer],
            recv_sem=whole_sem.at[me],
            device_id=(grp, peer),
            device_id_type=MESH,
        )

    def from_owner(peer):
        return pltpu.make_async_remote_copy(
            src_ref=whole.at[peer],
            dst_ref=whole.at[peer],
            send_sem=send_sem.at[peers + regions + peer],
            recv_sem=whole_sem.at[peer],
            device_id=(grp, peer),
            device_id_type=MESH,
        )

    def each(first, last, act):
        def step(i, _):
            act(i)
            return 0

        lax.fori_loop(first, last, step, 0)

    def start_term(step):
        peer, copy = to_owner(step)
        pl.when(peer < TAPS)(copy.start)

    each(1, peers, start_term)

    @pl.when(me < TAPS)
    def _():
        parts[me] = terms_ref[me]
        each(1, peers, lambda step: from_peer(step).wait_recv())
        mine = jnp.sum(parts[...], axis=0)
        part[...] = mine
        sums[grp] = mine
        each(1, regions, lambda step: to_region(step).start())
        each(1, regions, lambda step: from_region(step).wait_recv())
        whole[me] = jnp.sum(sums[...], axis=0)
        each(1, peers, lambda step: to_all(step).start())

    def take(owner):
        @pl.when(owner != me)
        def _():
            from_owner(owner).wait_recv()

    each(0, TAPS, take)

    def end_term(step):
        peer, copy = to_owner(step)
        pl.when(peer < TAPS)(copy.wait_send)

    each(1, peers, end_term)

    @pl.when(me < TAPS)
    def _():
        each(1, regions, lambda step: to_region(step).wait_send())
        each(1, peers, lambda step: to_all(step).wait_send())

    for k in range(TAPS):
        out_ref[k : k + 1, :] = whole[k]


def params(**more):
    return pltpu.CompilerParams(vmem_limit_bytes=48 * 2**20, **more)


def local(kernel, out_shape, scratch, *args):
    return pl.pallas_call(
        kernel,
        out_shape=out_shape,
        in_specs=[VMEM] * len(args),
        out_specs=jax.tree.map(lambda _: VMEM, out_shape),
        scratch_shapes=scratch,
        compiler_params=params(),
    )(*args)


def shape(dims, dtype=BF16):
    return jax.ShapeDtypeStruct(dims, dtype)


def total_terms(regions, peers, terms):
    return pl.pallas_call(
        functools.partial(reduce_kernel, regions, peers),
        out_shape=shape((TAPS, D), F32),
        in_specs=[VMEM],
        out_specs=VMEM,
        scratch_shapes=[
            pltpu.VMEM((peers, 1, D), F32),
            pltpu.VMEM((1, D), F32),
            pltpu.VMEM((regions, 1, D), F32),
            pltpu.VMEM((TAPS, 1, D), F32),
            pltpu.SemaphoreType.DMA((2 * peers + regions,)),
            pltpu.SemaphoreType.DMA((peers,)),
            pltpu.SemaphoreType.DMA((regions,)),
            pltpu.SemaphoreType.DMA((TAPS,)),
        ],
        compiler_params=params(collective_id=0, has_side_effects=True),
    )(terms)


def swap_rims(rims):
    count = lax.axis_size("grp")
    pairs = [(i, i + 1) for i in range(count - 1)]
    from_prev = lax.ppermute(rims[RIM:], "grp", pairs)
    from_next = lax.ppermute(rims[:RIM], "grp", [(b, a) for a, b in pairs])
    return from_prev, from_next


def on_device(features, cotangent, conv_weight, neighbours, halo_index, send_index, curve_slot):
    peers, slots = send_index.shape[1:]
    regions = lax.axis_size("grp")
    taps = neighbours.T
    send = send_index.reshape(1, peers * slots)
    curve = curve_slot.reshape(1, ROWS)
    lent = local(lend_kernel, shape((2 * RIM, D)), [], halo_index, features)
    from_prev, from_next = swap_rims(lent)
    padded = jnp.concatenate([features, from_prev, from_next], axis=0)
    outgoing = local(
        forward_kernel,
        shape((peers * slots, D)),
        [pltpu.VMEM((ROWS, D), F32)],
        taps,
        conv_weight,
        send,
        padded,
    )
    incoming = lax.all_to_all(outgoing, "pt", split_axis=0, concat_axis=0, tiled=True)
    filled = local(
        attention_kernel,
        shape((peers * slots, D)),
        [pltpu.VMEM((ROWS, D), BF16), pltpu.VMEM((ROWS, D), BF16)],
        curve,
        cotangent,
        incoming,
    )
    returned = lax.all_to_all(filled, "pt", split_axis=0, concat_axis=0, tiled=True)
    total, rims, terms = local(
        backward_kernel,
        (shape((ROWS, D), F32), shape((2 * RIM, D)), shape((TAPS, 1, D), F32)),
        [pltpu.VMEM((ROWS, D), BF16), pltpu.VMEM((TABLE, D), F32)],
        taps,
        conv_weight,
        send,
        padded,
        returned,
    )
    from_prev, from_next = swap_rims(rims)
    echoed = jnp.concatenate([from_prev, from_next], axis=0)
    grad_conv = total_terms(regions, peers, terms)
    grad_features = local(finish_kernel, shape((ROWS, D)), [], halo_index, total, echoed)
    return grad_features, grad_conv


def solution(mesh):
    in_specs = (
        P(("grp", "pt"), None),
        P(("grp", "pt"), None),
        P(),
        P(("grp", "pt"), None),
        P(("grp", "pt"), None),
        P(("grp", "pt"), None, None),
        P(("grp", "pt")),
    )
    out_specs = (P(("grp", "pt"), None), P())
    return jax.shard_map(
        on_device, mesh=mesh, in_specs=in_specs, out_specs=out_specs, check_vma=False
    )
```

time: 727 us -> 188 us (0.26); the launches traced: 716 us -> 188 us
  other arithmetic: 258 us -> 0.01 us
  local copies, waits for them, and re-layouts: 153 us -> 4.65 us
  matrix products: 123 us -> 0 us
  Pallas kernels: 0 us -> 95.4 us
  waiting for transfers between devices: 45 us -> 1.18 us
  blocking collectives: 99.9 us -> 64.5 us
  starting transfers between devices: 33.4 us -> 20.9 us
    scatter-add x29 -> x0, other arithmetic: 165 us -> none  [the longest x27 162 us: add_tap(): spread = spread.at[picked].add(conv_weight[kernel_tap] * grad_float)]
    gather x60 -> x0, local copies, waits for them, and re-layouts: 121 us -> none  [the longest x27 53.2 us: add_tap(): picked = padded[tap_index[:, kernel_tap]].astype(jnp.float32)]
    psum x1 -> x0, blocking collectives: 99.9 us -> none  [on_device(): grad_conv = lax.psum(terms, ('grp', 'pt'))]
    dot_general x64 -> x0, matrix products: 96.1 us -> none  [the longest x16 41.4 us: pair_grad(): jnp.einsum('hqk,qhd->khd', probs_low, upstream, preferred_element_type=jn...]
    pallas_call x0 -> x6, Pallas kernels: none -> 95.4 us  [the longest x5 68.1 us: local(): pl.pallas_call(kernel, out_shape=out_shape, in_specs=[VMEM] * len(args),...]
    all_to_all x0 -> x2, blocking collectives: none -> 64.5 us  [the longest x1 33.9 us: on_device(): lax.all_to_all(outgoing, 'pt', split_axis=0, concat_axis=0, tiled=True)]
    another operation x55 -> x0, other arithmetic: 57.7 us -> none
    all_to_all x2 -> x0, waiting for transfers between devices: 45 us -> none  [the longest x1 23.8 us: on_device(): lax.all_to_all(outgoing, 'pt', split_axis=0, concat_axis=0, tiled=True)]
  transfers between devices with their start and end apart: 6 -> 4, of which waited for: 2 -> 1; matrix products, arithmetic and copies ran while one was open for 2% -> 0% of each run, Pallas kernels for 0% -> 15%
where the time goes in v1:
time: 188 us
  Pallas kernels  95.4 us (51%)
  blocking collectives  64.5 us (34%)
  starting transfers between devices  20.9 us (11%)
  local copies, waits for them, and re-layouts  4.65 us (2%)
    pallas_call x5, Pallas kernels, local(): pl.pallas_call(kernel, out_shape=out_shape, in_specs=[VMEM] * len(args),...  68.1 us
    all_to_all x1, blocking collectives, on_device(): lax.all_to_all(outgoing, 'pt', split_axis=0, concat_axis=0, tiled=True)  33.9 us
    all_to_all x1, blocking collectives, on_device(): lax.all_to_all(filled, 'pt', split_axis=0, concat_axis=0, tiled=True)  30.6 us
    pallas_call x1, Pallas kernels, total_terms(): pl.pallas_call(functools.partial(reduce_kernel, regions, peers), out_shap...  27.3 us
    ppermute x2, starting transfers between devices, swap_rims(): from_next = lax.ppermute(rims[:RIM], 'grp', [(b, a) for a, b in pairs])  10.7 us
    ppermute x2, starting transfers between devices, swap_rims(): from_prev = lax.ppermute(rims[RIM:], 'grp', pairs)  10.2 us
    unnamed x21, local copies, waits for them, and re-layouts  4.54 us
  transfers between devices with their start and end apart: 4, of which 1 were waited for; matrix products, arithmetic and copies ran while one was open for 0% of the time, Pallas kernels for 15%

profile of v1, /device:TPU:1, one launch (start us, length us, event | category | flops | bytes accessed | tf_op | source)
XLA Modules:
  0.0 187.5 jit_solution(9116069604686604815)
XLA Ops:
  0.6 0.0 copy-start
  0.6 1.0 copy-done
  1.7 0.0 copy-start.5
  1.7 0.7 copy-done.5
  2.3 0.3 shard_map.86
  2.6 0.0 copy-start.8
  2.6 8.8 %collective-permute-start.1 = (bf16[64,512]{1,0:T(8,128)(2,1)S(1)}, bf16[64,512]{1,0:T(8,128)(2,1)S(1)}, u32[]{:S(2)}, u32[]{:S(2)}) collective-permute-start(bf16[64,512]{1,0:T(8,128)(2,1)S(1)} %get-tuple-element.10), channel_id=1, source_target_pairs={{32,0},{64,32},{96,64},{128,96},{160,128},{192,160},{224,192},{256... | collective-permute-start | bytes 196616 | tf_op jit(solution)/shard_map/ppermute | solution.py:303
  11.4 1.9 %collective-permute-start = (bf16[64,512]{1,0:T(8,128)(2,1)S(1)}, bf16[64,512]{1,0:T(8,128)(2,1)S(1)}, u32[]{:S(2)}, u32[]{:S(2)}) collective-permute-start(bf16[64,512]{1,0:T(8,128)(2,1)S(1)} %get-tuple-element.11), channel_id=1, source_target_pairs={{0,32},{32,64},{64,96},{96,128},{128,160},{160,192},{192,224},{224... | collective-permute-start | bytes 196616 | tf_op jit(solution)/shard_map/ppermute | solution.py:302
  13.4 0.0 copy-done.8
  13.4 0.1 reshape.14.send_ref
  13.4 0.0 copy-done.1
  13.5 1.2 collective-permute-done
  14.7 0.0 collective-permute-done.1
  14.7 0.8 copy-done.3
  15.5 0.0 copy-done.4
  15.5 17.1 %shard_map.87 = bf16[1024,512]{1,0:T(8,128)(2,1)S(1)} custom-call(s32[27,512]{1,0:T(8,128)S(1)} %bitcast.10, f32[27,512]{1,0:T(8,128)S(1)} %copy-done.4, s32[1,1024]{1,0:T(1,128)S(1)} %reshape.14.send_ref, bf16[640,512]{1,0:T(8,128)(2,1)S(1)} %constant_dynamic-update-slice_fusion.padded_ref), custom_call_target="tpu_custom_call" | custom-call | tf_op jit(solution)/shard_map/pallas_call | solution.py:265
  32.6 0.0 copy-start.2
  32.6 33.9 %all_to_all.22 = bf16[32,32,512]{2,1,0:T(8,128)(2,1)S(1)} all-to-all(bf16[32,32,512]{2,1,0:T(8,128)(2,1)S(1)} %bitcast.7), channel_id=1, replica_groups=mesh['grp'=16,'pt'=32] {'pt'}, dimensions={0} | all-to-all | bytes 2097152 | tf_op jit(solution)/shard_map/all_to_all | solution.py:325
  66.5 0.0 copy-done.2
  66.5 0.7 copy-done.7
  67.2 33.7 %shard_map.88 = bf16[1024,512]{1,0:T(8,128)(2,1)S(1)} custom-call(s32[1,512]{1,0:T(1,128)S(1)} %bitcast.12, bf16[512,512]{1,0:T(8,128)(2,1)S(1)} %copy-done.2, bf16[1024,512]{1,0:T(8,128)(2,1)S(1)} %bitcast.8), custom_call_target="tpu_custom_call" | custom-call | tf_op jit(solution)/shard_map/pallas_call | solution.py:265
  100.9 30.6 %all_to_all.23 = bf16[32,32,512]{2,1,0:T(8,128)(2,1)S(1)} all-to-all(bf16[32,32,512]{2,1,0:T(8,128)(2,1)S(1)} %bitcast.9), channel_id=1, replica_groups=mesh['grp'=16,'pt'=32] {'pt'}, dimensions={0} | all-to-all | bytes 2097152 | tf_op jit(solution)/shard_map/all_to_all | solution.py:334
  131.5 16.1 %shard_map.89 = (f32[512,512]{1,0:T(8,128)S(1)}, bf16[128,512]{1,0:T(8,128)(2,1)S(1)}, f32[27,1,512]{2,1,0:T(1,128)S(1)}) custom-call(s32[27,512]{1,0:T(8,128)S(1)} %bitcast.11, f32[27,512]{1,0:T(8,128)S(1)} %copy-done.4, s32[1,1024]{1,0:T(1,128)S(1)} %reshape.14.send_ref, bf16[640,512]{1,0:T(8,128)(2,1)S(1)} %constant_dynamic-update-slice_fusion.padded_ref, ...), custom_call_target="tpu_custom_call" | custom-call | tf_op jit(solution)/shard_map/pallas_call | solution.py:265
  147.6 8.3 %collective-permute-start.2 = (bf16[64,512]{1,0:T(8,128)(2,1)S(1)}, bf16[64,512]{1,0:T(8,128)(2,1)S(1)}, u32[]{:S(2)}, u32[]{:S(2)}) collective-permute-start(bf16[64,512]{1,0:T(8,128)(2,1)S(1)} %get-tuple-element.8), channel_id=1, source_target_pairs={{0,32},{32,64},{64,96},{96,128},{128,160},{160,192},{192,224},{224... | collective-permute-start | bytes 196616 | tf_op jit(solution)/shard_map/ppermute | solution.py:302
  155.9 1.9 %collective-permute-start.3 = (bf16[64,512]{1,0:T(8,128)(2,1)S(1)}, bf16[64,512]{1,0:T(8,128)(2,1)S(1)}, u32[]{:S(2)}, u32[]{:S(2)}) collective-permute-start(bf16[64,512]{1,0:T(8,128)(2,1)S(1)} %get-tuple-element.9), channel_id=1, source_target_pairs={{32,0},{64,32},{96,64},{128,96},{160,128},{192,160},{224,192},{256... | collective-permute-start | bytes 196616 | tf_op jit(solution)/shard_map/ppermute | solution.py:303
  157.8 27.3 %shard_map.91 = f32[27,512]{1,0:T(8,128)S(1)} custom-call(f32[27,1,512]{2,1,0:T(1,128)S(1)} %get-tuple-element.7.terms_ref), custom_call_target="tpu_custom_call" | custom-call | tf_op jit(solution)/shard_map/pallas_call | solution.py:280
  185.1 0.0 collective-permute-done.2
  185.1 0.0 collective-permute-done.3
  185.1 0.0 copy-start.6
  185.2 0.6 copy-done.6
  185.8 1.1 shard_map.90
  186.9 0.6 copy.12
  (10 shorter events, 0.1 us)
Async XLA Ops:
  0.6 1.0 copy-start
  1.7 0.7 copy-start.5
  2.3 11.1 %copy-start.1 = (bf16[512,512]{1,0:T(8,128)(2,1)S(1)}, bf16[512,512]{1,0:T(8,128)(2,1)}, u32[]{:S(2)}) copy-start(bf16[512,512]{1,0:T(8,128)(2,1)} %features_ref.1) | copy-start | bytes 1572868
  2.6 10.8 %copy-start.8 = (s32[1,32,32]{2,1,0:T(8,128)S(1)}, s32[1,32,32]{2,1,0:T(8,128)}, u32[]{:S(2)}) copy-start(s32[1,32,32]{2,1,0:T(8,128)} %param.12) | copy-start | bytes 12292
  2.6 12.1 %collective-permute-start.1 = (bf16[64,512]{1,0:T(8,128)(2,1)S(1)}, bf16[64,512]{1,0:T(8,128)(2,1)S(1)}, u32[]{:S(2)}, u32[]{:S(2)}) collective-permute-start(bf16[64,512]{1,0:T(8,128)(2,1)S(1)} %get-tuple-element.10), channel_id=1, source_target_pairs={{32,0},{64,32},{96,64},{128,96},{160,128},{192,160},{224,192},{256... | collective-permute-start | bytes 196616 | tf_op jit(solution)/shard_map/ppermute | solution.py:303
  11.4 3.2 %collective-permute-start = (bf16[64,512]{1,0:T(8,128)(2,1)S(1)}, bf16[64,512]{1,0:T(8,128)(2,1)S(1)}, u32[]{:S(2)}, u32[]{:S(2)}) collective-permute-start(bf16[64,512]{1,0:T(8,128)(2,1)S(1)} %get-tuple-element.11), channel_id=1, source_target_pairs={{0,32},{32,64},{64,96},{96,128},{128,160},{160,192},{192,224},{224... | collective-permute-start | bytes 196616 | tf_op jit(solution)/shard_map/ppermute | solution.py:302
  14.7 0.8 copy-start.3
  14.7 0.9 copy-start.4
  32.6 33.9 %copy-start.2 = (bf16[512,512]{1,0:T(8,128)(2,1)S(1)}, bf16[512,512]{1,0:T(8,128)(2,1)}, u32[]{:S(2)}) copy-start(bf16[512,512]{1,0:T(8,128)(2,1)} %cotangent_ref.1) | copy-start | bytes 1572868
  66.5 0.7 copy-start.7
  147.6 37.5 %collective-permute-start.2 = (bf16[64,512]{1,0:T(8,128)(2,1)S(1)}, bf16[64,512]{1,0:T(8,128)(2,1)S(1)}, u32[]{:S(2)}, u32[]{:S(2)}) collective-permute-start(bf16[64,512]{1,0:T(8,128)(2,1)S(1)} %get-tuple-element.8), channel_id=1, source_target_pairs={{0,32},{32,64},{64,96},{96,128},{128,160},{160,192},{192,224},{224... | collective-permute-start | bytes 196616 | tf_op jit(solution)/shard_map/ppermute | solution.py:302
  155.9 29.2 %collective-permute-start.3 = (bf16[64,512]{1,0:T(8,128)(2,1)S(1)}, bf16[64,512]{1,0:T(8,128)(2,1)S(1)}, u32[]{:S(2)}, u32[]{:S(2)}) collective-permute-start(bf16[64,512]{1,0:T(8,128)(2,1)S(1)} %get-tuple-element.9), channel_id=1, source_target_pairs={{32,0},{64,32},{96,64},{128,96},{160,128},{192,160},{224,192},{256... | collective-permute-start | bytes 196616 | tf_op jit(solution)/shard_map/ppermute | solution.py:303
  185.1 0.7 copy-start.6

commit v2 on v1

v2 whole, which is shorter than its diff:
```python
import functools

import jax
import jax.numpy as jnp
from jax import lax
from jax.experimental import pallas as pl
from jax.experimental.pallas import tpu as pltpu
from jax.sharding import PartitionSpec as P

D = 512
ROWS = 512
RIM = 64
TABLE = ROWS + 2 * RIM
TAPS = 27
CENTRE = TAPS // 2
HEAD_DIM = 16
LANES = 128
HALF = D // 2
BF16 = jnp.bfloat16
F32 = jnp.float32
I16 = jnp.int16
VMEM = pl.BlockSpec(memory_space=pltpu.VMEM)
MESH = pl.DeviceIdType.MESH


def dot(a, b, dims=((1,), (0,))):
    return lax.dot_general(a, b, (dims, ((), ())), preferred_element_type=F32)


def pick(mask):
    return jnp.where(mask, jnp.ones((), BF16), jnp.zeros((), BF16))


def rows_of(index_row, width):
    count = index_row.shape[1]
    column = jnp.broadcast_to(index_row, (LANES, count)).T.astype(I16)
    lane = lax.broadcasted_iota(jnp.int32, (count, LANES), 1).astype(I16)
    blocks = [pick(column == lane + jnp.asarray(start, I16)) for start in range(0, width, LANES)]
    return jnp.concatenate(blocks, axis=1)


def columns_of(index_row, height):
    count = index_row.shape[1]
    row = jnp.broadcast_to(index_row, (16, count)).astype(I16)
    sub = lax.broadcasted_iota(jnp.int32, (16, count), 0).astype(I16)
    blocks = [pick(row == sub + jnp.asarray(start, I16)) for start in range(0, height, 16)]
    return jnp.concatenate(blocks, axis=0)


def other_tap(step):
    return jnp.where(step < CENTRE, step, step + 1)


def each(first, last, act):
    def step(i, _):
        act(i)
        return 0

    lax.fori_loop(first, last, step, 0)


def head_grads(rows, cot):
    scaled = rows * jnp.asarray(HEAD_DIM**-0.5, BF16)
    head_of = lax.broadcasted_iota(jnp.int32, (ROWS, LANES), 1) // HEAD_DIM
    total = cot.astype(F32)
    for h in range(LANES // HEAD_DIM):
        inside = head_of == h
        keys = jnp.where(inside, rows, jnp.zeros((), BF16))
        scores = dot(keys, scaled, ((1,), (1,)))
        dprobs = dot(keys, cot, ((1,), (1,)))
        weights = jnp.exp(scores - jnp.max(scores, axis=0, keepdims=True))
        probs = weights * (1.0 / jnp.sum(weights, axis=0, keepdims=True))
        delta = jnp.sum(probs * dprobs, axis=0, keepdims=True)
        dscores = (probs * (dprobs - delta)).astype(BF16)
        grads = dot(probs.astype(BF16), cot) + dot(dscores, scaled)
        grads = grads + dot(dscores, scaled, ((0,), (0,)))
        total = total + jnp.where(inside, grads, 0.0)
    return total.astype(BF16)


def kernel(
    regions,
    peers,
    slots,
    taps_ref,
    weight_ref,
    send_ref,
    curve_ref,
    halo_ref,
    features_ref,
    cotangent_ref,
    out_ref,
    conv_ref,
    padded,
    lent,
    tap_rows,
    tap_columns,
    send_rows,
    send_columns,
    curve_rows,
    curve_columns,
    acc,
    outgoing,
    incoming,
    curve,
    grads,
    filled,
    returned,
    grad_hidden,
    spread,
    total,
    rims,
    echoed,
    terms,
    parts,
    part,
    sums,
    whole,
    halo_sems,
    echo_sems,
    out_sems,
    in_sems,
    filled_sems,
    returned_sems,
    term_sems,
    part_sems,
    sum_sems,
    whole_sems,
):
    grp = lax.axis_index("grp")
    me = lax.axis_index("pt")
    flat = peers * slots
    barrier = pltpu.get_barrier_semaphore()

    def greet_peer(step):
        peer = (me + step) % peers
        pl.semaphore_signal(barrier, inc=1, device_id=(grp, peer), device_id_type=MESH)

    def greet_region(step):
        other = (grp + step) % regions
        pl.semaphore_signal(barrier, inc=1, device_id=(other, me), device_id_type=MESH)

    each(1, peers, greet_peer)
    each(1, regions, greet_region)

    def rim_copies(source, target, sems, to_prev, to_next):
        prev = pltpu.make_async_remote_copy(
            src_ref=source.at[pl.ds(0, RIM)],
            dst_ref=target.at[pl.ds(to_prev, RIM)],
            send_sem=sems.at[0],
            recv_sem=sems.at[1],
            device_id=((grp + regions - 1) % regions, me),
            device_id_type=MESH,
        )
        next_ = pltpu.make_async_remote_copy(
            src_ref=source.at[pl.ds(RIM, RIM)],
            dst_ref=target.at[pl.ds(to_next, RIM)],
            send_sem=sems.at[2],
            recv_sem=sems.at[3],
            device_id=((grp + 1) % regions, me),
            device_id_type=MESH,
        )
        return prev, next_

    def start_rims(copies):
        pl.when(grp > 0)(copies[0].start)
        pl.when(grp < regions - 1)(copies[1].start)

    def take_rims(copies):
        pl.when(grp < regions - 1)(copies[0].wait_recv)
        pl.when(grp > 0)(copies[1].wait_recv)

    def end_rims(copies):
        pl.when(grp > 0)(copies[0].wait_send)
        pl.when(grp < regions - 1)(copies[1].wait_send)

    lent[...] = dot(rows_of(halo_ref[...], ROWS), features_ref[...]).astype(BF16)
    padded[:ROWS, :] = features_ref[...]

    @pl.when(grp == 0)
    def _():
        padded[ROWS : ROWS + RIM, :] = jnp.zeros((RIM, D), BF16)
        echoed[:RIM, :] = jnp.zeros((RIM, D), BF16)

    @pl.when(grp == regions - 1)
    def _():
        padded[ROWS + RIM :, :] = jnp.zeros((RIM, D), BF16)
        echoed[RIM:, :] = jnp.zeros((RIM, D), BF16)

    pl.semaphore_wait(barrier, peers - 1 + regions - 1)
    halo = rim_copies(lent, padded, halo_sems, ROWS + RIM, ROWS)
    start_rims(halo)

    def build_rows(step):
        k = other_tap(step)
        tap_rows[k] = rows_of(taps_ref[pl.ds(k, 1), :], TABLE)

    each(0, TAPS - 1, build_rows)
    send_rows[...] = rows_of(send_ref[...], ROWS)
    take_rims(halo)

    def send_block(source, target, send_sem, recv_sem, lanes):
        def one(step):
            peer = (me + step) % peers
            pltpu.make_async_remote_copy(
                src_ref=source.at[peer, :, lanes],
                dst_ref=target.at[me, :, lanes],
                send_sem=send_sem,
                recv_sem=recv_sem,
                device_id=(grp, peer),
                device_id_type=MESH,
            ).start()

        each(1, peers, one)
        target[me, :, lanes] = source[me, :, lanes]

    def wait_blocks(buffer, sem, lanes):
        view = buffer.at[pl.ds(0, peers - 1), :, lanes]
        pltpu.make_async_copy(view, view, sem).wait()

    everything = pl.ds(0, HALF)

    def forward(half):
        span = pl.ds(pl.multiple_of(half * HALF, HALF), HALF)
        own = padded[:ROWS, span].astype(F32)
        acc[...] = own + own * weight_ref[CENTRE : CENTRE + 1, span]

        def tap(step):
            k = other_tap(step)
            acc[...] += dot(tap_rows[k], padded[:, span]) * weight_ref[pl.ds(k, 1), span]

        each(0, TAPS - 1, tap)
        hidden = acc[...].astype(BF16)
        outgoing[half] = dot(send_rows[...], hidden).astype(BF16).reshape(peers, slots, HALF)
        send_block(outgoing.at[half], incoming.at[half], out_sems.at[half], in_sems.at[half], everything)

    each(0, 2, forward)

    def build_columns(step):
        k = other_tap(step)
        tap_columns[k] = columns_of(taps_ref[pl.ds(k, 1), :], TABLE)

    each(0, TAPS - 1, build_columns)
    curve_rows[...] = rows_of(curve_ref[...], flat)
    curve_columns[...] = columns_of(curve_ref[...], flat)
    send_columns[...] = columns_of(send_ref[...], ROWS)

    def attend(half):
        wait_blocks(incoming.at[half], in_sems.at[half], everything)
        curve[...] = dot(curve_rows[...], incoming[half].reshape(flat, HALF)).astype(BF16)

        def group(part_of):
            lanes = pl.ds(pl.multiple_of(part_of * LANES, LANES), LANES)
            span = pl.ds(pl.multiple_of(half * HALF + part_of * LANES, LANES), LANES)
            grads[...] = head_grads(curve[:, lanes], cotangent_ref[:, span])
            placed = dot(curve_columns[...], grads[...]).astype(BF16)
            filled[half, :, :, lanes] = placed.reshape(peers, slots, LANES)
            index = half * 2 + part_of
            send_block(
                filled.at[half], returned.at[half], filled_sems.at[index], returned_sems.at[index], lanes
            )

        each(0, 2, group)

    each(0, 2, attend)

    def backward(half):
        span = pl.ds(pl.multiple_of(half * HALF, HALF), HALF)
        for part_of in range(2):
            lanes = pl.ds(part_of * LANES, LANES)
            wait_blocks(returned.at[half], returned_sems.at[half * 2 + part_of], lanes)
        grad_hidden[...] = dot(send_columns[...], returned[half].reshape(flat, HALF)).astype(BF16)
        grad = grad_hidden[...].astype(F32)
        spread[:ROWS, :] = grad + grad * weight_ref[CENTRE : CENTRE + 1, span]
        spread[ROWS:, :] = jnp.zeros((2 * RIM, HALF), F32)
        terms[CENTRE, :, span] = jnp.sum(grad * padded[:ROWS, span].astype(F32), axis=0, keepdims=True)

        def tap(step):
            k = other_tap(step)
            landed = dot(tap_columns[k], grad_hidden[...])
            spread[...] += landed * weight_ref[pl.ds(k, 1), span]
            terms[k, :, span] = jnp.sum(landed * padded[:, span].astype(F32), axis=0, keepdims=True)

        each(0, TAPS - 1, tap)
        total[:, span] = spread[:ROWS, :]
        rims[:, span] = spread[ROWS:, :].astype(BF16)

    each(0, 2, backward)

    echo = rim_copies(rims, echoed, echo_sems, RIM, 0)
    start_rims(echo)

    def to_owner(step):
        peer = (me + step) % peers
        return peer, pltpu.make_async_remote_copy(
            src_ref=terms.at[peer % TAPS],
            dst_ref=parts.at[me],
            send_sem=term_sems.at[peer],
            recv_sem=part_sems.at[me],
            device_id=(grp, peer),
            device_id_type=MESH,
        )

    def from_peer(step):
        peer = (me + peers - step) % peers
        return pltpu.make_async_remote_copy(
            src_ref=terms.at[0],
            dst_ref=parts.at[peer],
            send_sem=term_sems.at[peer],
            recv_sem=part_sems.at[peer],
            device_id=(grp, peer),
            device_id_type=MESH,
        )

    def to_region(step):
        other = (grp + step) % regions
        return pltpu.make_async_remote_copy(
            src_ref=part,
            dst_ref=sums.at[grp],
            send_sem=term_sems.at[peers + other],
            recv_sem=sum_sems.at[grp],
            device_id=(other, me),
            device_id_type=MESH,
        )

    def from_region(step):
        other = (grp + regions - step) % regions
        return pltpu.make_async_remote_copy(
            src_ref=part,
            dst_ref=sums.at[other],
            send_sem=term_sems.at[peers + other],
            recv_sem=sum_sems.at[other],
            device_id=(other, me),
            device_id_type=MESH,
        )

    def to_all(step):
        peer = (me + step) % peers
        return pltpu.make_async_remote_copy(
            src_ref=whole.at[me],
            dst_ref=whole.at[me],
            send_sem=term_sems.at[peers + regions + peer],
            recv_sem=whole_sems.at[me],
            device_id=(grp, peer),
            device_id_type=MESH,
        )

    def from_owner(peer):
        return pltpu.make_async_remote_copy(
            src_ref=whole.at[peer],
            dst_ref=whole.at[peer],
            send_sem=term_sems.at[peers + regions + peer],
            recv_sem=whole_sems.at[peer],
            device_id=(grp, peer),
            device_id_type=MESH,
        )

    def start_term(step):
        peer, copy = to_owner(step)
        pl.when(peer < TAPS)(copy.start)

    each(1, peers, start_term)

    take_rims(echo)
    out_ref[...] = (total[...] + dot(columns_of(halo_ref[...], ROWS), echoed[...])).astype(BF16)

    @pl.when(me < TAPS)
    def _():
        parts[me] = terms[me]
        each(1, peers, lambda step: from_peer(step).wait_recv())
        mine = jnp.sum(parts[...], axis=0)
        part[...] = mine
        sums[grp] = mine
        each(1, regions, lambda step: to_region(step).start())
        each(1, regions, lambda step: from_region(step).wait_recv())
        whole[me] = jnp.sum(sums[...], axis=0)
        each(1, peers, lambda step: to_all(step).start())

    end_rims(halo)
    end_rims(echo)
    for half in range(2):
        wait_blocks(outgoing.at[half], out_sems.at[half], everything)
        for part_of in range(2):
            lanes = pl.ds(part_of * LANES, LANES)
            wait_blocks(filled.at[half], filled_sems.at[half * 2 + part_of], lanes)

    def take(owner):
        @pl.when(owner != me)
        def _():
            from_owner(owner).wait_recv()

    each(0, TAPS, take)

    def end_term(step):
        peer, copy = to_owner(step)
        pl.when(peer < TAPS)(copy.wait_send)

    each(1, peers, end_term)

    @pl.when(me < TAPS)
    def _():
        each(1, regions, lambda step: to_region(step).wait_send())
        each(1, peers, lambda step: to_all(step).wait_send())

    for k in range(TAPS):
        conv_ref[k : k + 1, :] = whole[k]


def on_device(features, cotangent, conv_weight, neighbours, halo_index, send_index, curve_slot):
    peers, slots = send_index.shape[1:]
    regions = lax.axis_size("grp")
    flat = peers * slots
    args = (
        neighbours.T,
        conv_weight,
        send_index.reshape(1, flat),
        curve_slot.reshape(1, ROWS),
        halo_index,
        features,
        cotangent,
    )
    blocks = pltpu.VMEM((2, peers, slots, HALF), BF16)
    dma = pltpu.SemaphoreType.DMA
    return pl.pallas_call(
        functools.partial(kernel, regions, peers, slots),
        out_shape=(
            jax.ShapeDtypeStruct((ROWS, D), BF16),
            jax.ShapeDtypeStruct((TAPS, D), F32),
        ),
        in_specs=[VMEM] * len(args),
        out_specs=(VMEM, VMEM),
        scratch_shapes=[
            pltpu.VMEM((TABLE, D), BF16),
            pltpu.VMEM((2 * RIM, D), BF16),
            pltpu.VMEM((TAPS, ROWS, TABLE), BF16),
            pltpu.VMEM((TAPS, TABLE, ROWS), BF16),
            pltpu.VMEM((flat, ROWS), BF16),
            pltpu.VMEM((ROWS, flat), BF16),
            pltpu.VMEM((ROWS, flat), BF16),
            pltpu.VMEM((flat, ROWS), BF16),
            pltpu.VMEM((ROWS, HALF), F32),
            blocks,
            blocks,
            pltpu.VMEM((ROWS, HALF), BF16),
            pltpu.VMEM((ROWS, LANES), BF16),
            blocks,
            blocks,
            pltpu.VMEM((ROWS, HALF), BF16),
            pltpu.VMEM((TABLE, HALF), F32),
            pltpu.VMEM((ROWS, D), F32),
            pltpu.VMEM((2 * RIM, D), BF16),
            pltpu.VMEM((2 * RIM, D), BF16),
            pltpu.VMEM((TAPS, 1, D), F32),
            pltpu.VMEM((peers, 1, D), F32),
            pltpu.VMEM((1, D), F32),
            pltpu.VMEM((regions, 1, D), F32),
            pltpu.VMEM((TAPS, 1, D), F32),
            dma((4,)),
            dma((4,)),
            dma((2,)),
            dma((2,)),
            dma((4,)),
            dma((4,)),
            dma((2 * peers + regions,)),
            dma((peers,)),
            dma((regions,)),
            dma((TAPS,)),
        ],
        compiler_params=pltpu.CompilerParams(
            vmem_limit_bytes=60 * 2**20, collective_id=0, has_side_effects=True
        ),
    )(*args)


def solution(mesh):
    in_specs = (
        P(("grp", "pt"), None),
        P(("grp", "pt"), None),
        P(),
        P(("grp", "pt"), None),
        P(("grp", "pt"), None),
        P(("grp", "pt"), None, None),
        P(("grp", "pt")),
    )
    out_specs = (P(("grp", "pt"), None), P())
    return jax.shard_map(
        on_device, mesh=mesh, in_specs=in_specs, out_specs=out_specs, check_vma=False
    )
```

time: 188 us -> 124 us (0.66)
  blocking collectives: 64.5 us -> 0 us
  Pallas kernels: 95.4 us -> 120 us
  starting transfers between devices: 20.9 us -> 0 us
    all_to_all x2 -> x0, blocking collectives: 64.5 us -> none  [the longest x1 33.9 us: on_device(): lax.all_to_all(outgoing, 'pt', split_axis=0, concat_axis=0, tiled=True)]
    pallas_call x6 -> x1, Pallas kernels: 95.4 us -> 120 us  [on_device(): pl.pallas_call(functools.partial(kernel, regions, peers, slots), out_shap...]
    ppermute x4 -> x0, starting transfers between devices: 20.9 us -> none  [the longest x2 10.7 us: swap_rims(): from_next = lax.ppermute(rims[:RIM], 'grp', [(b, a) for a, b in pairs])]
    unnamed x21 -> x4, local copies, waits for them, and re-layouts: 4.54 us -> 2.53 us
  transfers between devices with their start and end apart: 4 -> 0, of which waited for: 1 -> 0; matrix products, arithmetic and copies ran while one was open for 0% -> 0% of each run, Pallas kernels for 15% -> 0%
where the time goes in v2:
time: 124 us
  Pallas kernels  120 us (97%)
  local copies, waits for them, and re-layouts  3.92 us (3%)
    pallas_call x1, Pallas kernels, on_device(): pl.pallas_call(functools.partial(kernel, regions, peers, slots), out_shap...  120 us
    unnamed x4, local copies, waits for them, and re-layouts  2.53 us

profile of v2, /device:TPU:1, one launch (start us, length us, event | category | flops | bytes accessed | tf_op | source)
XLA Modules:
  0.0 124.3 jit_solution(12829447355889703476)
XLA Ops:
  0.6 1.4 %reshape.10.send_ref = s32[1,1024]{1,0:T(1,128)} reshape(s32[1,32,32]{2,1,0:T(8,128)} %param.12) | data formatting | bytes 8192 | tf_op jit(solution)/shard_map/reshape | solution.py:416
  2.0 119.7 %shard_map.86 = (bf16[512,512]{1,0:T(8,128)(2,1)}, f32[27,512]{1,0:T(8,128)}) custom-call(s32[27,512]{1,0:T(8,128)} %bitcast.2, f32[27,512]{1,0:T(8,128)} %weight_ref.1, s32[1,1024]{1,0:T(1,128)} %reshape.10.send_ref, s32[1,512]{1,0:T(1,128)} %bitcast.3, s32[1,128]{1,0:T(1,128)} %halo_ref.1, bf16[512,512]{1,0:T(8,128)(2,1)} %features_ref.1, ...), custom_call_target="tpu_custom_call" | custom-call | tf_op jit(solution)/shard_map/pallas_call | solution.py:424
  121.7 0.0 copy-start
  121.7 1.9 %copy.11 = bf16[512,512]{1,0:T(8,128)(2,1)} copy(bf16[512,512]{1,0:T(8,128)(2,1)} %get-tuple-element.4) | data formatting | bytes 1048576
  123.6 0.0 copy-done
  123.6 0.6 copy.12
Async XLA Ops:
  121.7 1.9 %copy-start = (f32[27,512]{1,0:T(8,128)S(1)}, f32[27,512]{1,0:T(8,128)}, u32[]{:S(2)}) copy-start(f32[27,512]{1,0:T(8,128)} %get-tuple-element.5) | copy-start | bytes 165892

commit v3 on v2

v3 whole, which is shorter than its diff:
```python
import functools

import jax
import jax.numpy as jnp
from jax import lax
from jax.experimental import pallas as pl
from jax.experimental.pallas import tpu as pltpu
from jax.sharding import PartitionSpec as P

D = 512
ROWS = 512
RIM = 64
TABLE = ROWS + 2 * RIM
TAPS = 27
CENTRE = TAPS // 2
HEAD_DIM = 16
LANES = 128
HALF = D // 2
BF16 = jnp.bfloat16
F32 = jnp.float32
I16 = jnp.int16
VMEM = pl.BlockSpec(memory_space=pltpu.VMEM)
MESH = pl.DeviceIdType.MESH


def dot(a, b, dims=((1,), (0,))):
    return lax.dot_general(a, b, (dims, ((), ())), preferred_element_type=F32)


def pick(mask):
    return jnp.where(mask, jnp.ones((), BF16), jnp.zeros((), BF16))


def rows_of(index_row, width):
    count = index_row.shape[1]
    column = jnp.broadcast_to(index_row, (LANES, count)).T.astype(I16)
    lane = lax.broadcasted_iota(jnp.int32, (count, LANES), 1).astype(I16)
    blocks = [pick(column == lane + jnp.asarray(start, I16)) for start in range(0, width, LANES)]
    return jnp.concatenate(blocks, axis=1)


def columns_of(index_row, height):
    count = index_row.shape[1]
    row = jnp.broadcast_to(index_row, (16, count)).astype(I16)
    sub = lax.broadcasted_iota(jnp.int32, (16, count), 0).astype(I16)
    blocks = [pick(row == sub + jnp.asarray(start, I16)) for start in range(0, height, 16)]
    return jnp.concatenate(blocks, axis=0)


def each(first, last, act):
    def step(i, _):
        act(i)
        return 0

    lax.fori_loop(first, last, step, 0)


def softmax_grads(scores, dprobs):
    weights = jnp.exp(scores - jnp.max(scores, axis=0, keepdims=True))
    inverse = 1.0 / jnp.sum(weights, axis=0, keepdims=True)
    delta = jnp.sum(weights * dprobs, axis=0, keepdims=True) * inverse
    probs = weights * inverse
    return probs.astype(BF16), (probs * (dprobs - delta)).astype(BF16)


def head_grads(rows, cot):
    scaled = rows * jnp.asarray(HEAD_DIM**-0.5, BF16)
    head_of = lax.broadcasted_iota(jnp.int32, (ROWS, LANES), 1) // HEAD_DIM
    heads = LANES // HEAD_DIM

    def products(h):
        keys = jnp.where(head_of == h, rows, jnp.zeros((), BF16))
        queries = [slice(start, start + LANES) for start in range(0, ROWS, LANES)]
        return [
            (dot(keys, scaled[at], ((1,), (1,))), dot(keys, cot[at], ((1,), (1,)))) for at in queries
        ]

    total = cot.astype(F32)
    ahead = products(0)
    for h in range(heads):
        now = ahead
        if h + 1 < heads:
            ahead = products(h + 1)
        pairs = [softmax_grads(*pair) for pair in now]
        probs = jnp.concatenate([pair[0] for pair in pairs], axis=1)
        dscores = jnp.concatenate([pair[1] for pair in pairs], axis=1)
        grads = dot(probs, cot) + dot(dscores, scaled) + dot(dscores, scaled, ((0,), (0,)))
        total = total + jnp.where(head_of == h, grads, 0.0)
    return total.astype(BF16)


def kernel(
    regions,
    peers,
    slots,
    taps_ref,
    weight_ref,
    send_ref,
    curve_ref,
    halo_ref,
    features_ref,
    cotangent_ref,
    out_ref,
    conv_ref,
    padded,
    lent,
    send_rows,
    send_columns,
    curve_rows,
    curve_columns,
    acc,
    outgoing,
    incoming,
    curve,
    grads,
    filled,
    returned,
    grad_hidden,
    spread,
    total,
    rims,
    echoed,
    terms,
    parts,
    part,
    sums,
    whole,
    halo_sems,
    echo_sems,
    out_sems,
    in_sems,
    filled_sems,
    returned_sems,
    part_sems,
    sum_sems,
    whole_sems,
):
    grp = lax.axis_index("grp")
    me = lax.axis_index("pt")
    flat = peers * slots
    share = parts.shape[1]
    send_row = jnp.concatenate([send_ref[p : p + 1, :] for p in range(peers)], axis=1)
    barrier = pltpu.get_barrier_semaphore()

    def greet_peer(step):
        peer = (me + step) % peers
        pl.semaphore_signal(barrier, inc=1, device_id=(grp, peer), device_id_type=MESH)

    def greet_region(step):
        other = (grp + step) % regions
        pl.semaphore_signal(barrier, inc=1, device_id=(other, me), device_id_type=MESH)

    each(1, peers, greet_peer)
    each(1, regions, greet_region)

    def rim_copies(source, target, sems, to_prev, to_next):
        prev = pltpu.make_async_remote_copy(
            src_ref=source.at[pl.ds(0, RIM)],
            dst_ref=target.at[pl.ds(to_prev, RIM)],
            send_sem=sems.at[0],
            recv_sem=sems.at[1],
            device_id=((grp + regions - 1) % regions, me),
            device_id_type=MESH,
        )
        next_ = pltpu.make_async_remote_copy(
            src_ref=source.at[pl.ds(RIM, RIM)],
            dst_ref=target.at[pl.ds(to_next, RIM)],
            send_sem=sems.at[2],
            recv_sem=sems.at[3],
            device_id=((grp + 1) % regions, me),
            device_id_type=MESH,
        )
        return prev, next_

    def start_rims(copies):
        pl.when(grp > 0)(copies[0].start)
        pl.when(grp < regions - 1)(copies[1].start)

    def take_rims(copies):
        pl.when(grp < regions - 1)(copies[0].wait_recv)
        pl.when(grp > 0)(copies[1].wait_recv)

    def end_rims(copies):
        pl.when(grp > 0)(copies[0].wait_send)
        pl.when(grp < regions - 1)(copies[1].wait_send)

    terms[TAPS:] = jnp.zeros((regions * share - TAPS, 1, D), F32)
    lent[...] = dot(rows_of(halo_ref[...], ROWS), features_ref[...]).astype(BF16)
    padded[:ROWS, :] = features_ref[...]

    @pl.when(grp == 0)
    def _():
        padded[ROWS : ROWS + RIM, :] = jnp.zeros((RIM, D), BF16)
        echoed[:RIM, :] = jnp.zeros((RIM, D), BF16)

    @pl.when(grp == regions - 1)
    def _():
        padded[ROWS + RIM :, :] = jnp.zeros((RIM, D), BF16)
        echoed[RIM:, :] = jnp.zeros((RIM, D), BF16)

    def weighted(step, half, one_hot, table):
        span = pl.ds(pl.multiple_of(half * HALF, HALF), HALF)
        added = jnp.zeros((ROWS, HALF), F32)
        for k in range(CENTRE):
            k = step * (CENTRE + 1) + k
            picked = dot(one_hot(taps_ref[pl.ds(k, 1), :]), table[:, span])
            added = added + picked * weight_ref[pl.ds(k, 1), span]
        return added

    def from_own(half):
        span = pl.ds(pl.multiple_of(half * HALF, HALF), HALF)
        own = padded[:ROWS, span].astype(F32)
        acc[half] = own + own * weight_ref[CENTRE : CENTRE + 1, span]

        def taps(step):
            acc[half] += weighted(step, half, lambda row: rows_of(row, ROWS), padded.at[pl.ds(0, ROWS)])

        each(0, 2, taps)

    each(0, 2, from_own)
    pl.semaphore_wait(barrier, peers - 1 + regions - 1)
    halo = rim_copies(lent, padded, halo_sems, ROWS + RIM, ROWS)
    start_rims(halo)
    send_rows[...] = rows_of(send_row, ROWS)
    send_columns[...] = columns_of(send_row, ROWS)
    curve_rows[...] = rows_of(curve_ref[...], flat)
    curve_columns[...] = columns_of(curve_ref[...], flat)
    take_rims(halo)

    def send_block(source, target, send_sem, recv_sem, lanes):
        def one(step):
            peer = (me + step) % peers
            pltpu.make_async_remote_copy(
                src_ref=source.at[peer, :, lanes],
                dst_ref=target.at[me, :, lanes],
                send_sem=send_sem,
                recv_sem=recv_sem,
                device_id=(grp, peer),
                device_id_type=MESH,
            ).start()

        each(1, peers, one)
        target[me, :, lanes] = source[me, :, lanes]

    def wait_blocks(buffer, sem, lanes):
        view = buffer.at[pl.ds(0, peers - 1), :, lanes]
        pltpu.make_async_copy(view, view, sem).wait()

    def forward(half):
        def taps(step):
            acc[half] += weighted(
                step, half, lambda row: rows_of(row - ROWS, 2 * RIM), padded.at[pl.ds(ROWS, 2 * RIM)]
            )

        each(0, 2, taps)
        hidden = acc[half].astype(BF16)
        outgoing[half] = dot(send_rows[...], hidden).astype(BF16).reshape(peers, slots, HALF)

        def group(part_of):
            lanes = pl.ds(pl.multiple_of(part_of * LANES, LANES), LANES)
            index = half * 2 + part_of
            send_block(outgoing.at[half], incoming.at[half], out_sems.at[index], in_sems.at[index], lanes)

        each(0, 2, group)

    each(0, 2, forward)

    def attend(index):
        half = index // 2
        lanes = pl.ds(pl.multiple_of(index % 2 * LANES, LANES), LANES)
        span = pl.ds(pl.multiple_of(index * LANES, LANES), LANES)
        wait_blocks(incoming.at[half], in_sems.at[index], lanes)
        rows = incoming[half, :, :, lanes].reshape(flat, LANES)
        curve[...] = dot(curve_rows[...], rows).astype(BF16)
        grads[...] = head_grads(curve[...], cotangent_ref[:, span])
        placed = dot(curve_columns[...], grads[...]).astype(BF16)
        filled[half, :, :, lanes] = placed.reshape(peers, slots, LANES)
        send_block(filled.at[half], returned.at[half], filled_sems.at[index], returned_sems.at[index], lanes)

    each(0, 4, attend)

    def backward(half):
        span = pl.ds(pl.multiple_of(half * HALF, HALF), HALF)
        for part_of in range(2):
            lanes = pl.ds(part_of * LANES, LANES)
            wait_blocks(returned.at[half], returned_sems.at[half * 2 + part_of], lanes)
        grad_hidden[...] = dot(send_columns[...], returned[half].reshape(flat, HALF)).astype(BF16)
        grad = grad_hidden[...].astype(F32)
        spread[:ROWS, :] = grad + grad * weight_ref[CENTRE : CENTRE + 1, span]
        spread[ROWS:, :] = jnp.zeros((2 * RIM, HALF), F32)
        terms[CENTRE, :, span] = jnp.sum(grad * padded[:ROWS, span].astype(F32), axis=0, keepdims=True)

        def taps(step):
            added = jnp.zeros((TABLE, HALF), F32)
            for k in range(CENTRE):
                k = step * (CENTRE + 1) + k
                landed = dot(columns_of(taps_ref[pl.ds(k, 1), :], TABLE), grad_hidden[...])
                terms[k, :, span] = jnp.sum(landed * padded[:, span].astype(F32), axis=0, keepdims=True)
                added = added + landed * weight_ref[pl.ds(k, 1), span]
            spread[...] += added

        each(0, 2, taps)
        total[:, span] = spread[:ROWS, :]
        rims[:, span] = spread[ROWS:, :].astype(BF16)

    each(0, 2, backward)

    echo = rim_copies(rims, echoed, echo_sems, RIM, 0)
    start_rims(echo)

    def over_regions(source, target, sems):
        def one(step):
            other = (grp + step) % regions
            pltpu.make_async_remote_copy(
                src_ref=source(other),
                dst_ref=target.at[grp],
                send_sem=sems.at[0],
                recv_sem=sems.at[1],
                device_id=(other, me),
                device_id_type=MESH,
            ).start()

        each(1, regions, one)

    def wait_rows(buffer, sem, count):
        view = buffer.at[pl.ds(0, count)]
        pltpu.make_async_copy(view, view, sem).wait()

    over_regions(lambda other: terms.at[pl.ds(other * share, share)], parts, part_sems)

    take_rims(echo)
    out_ref[...] = (total[...] + dot(columns_of(halo_ref[...], ROWS), echoed[...])).astype(BF16)

    parts[grp] = terms[pl.ds(grp * share, share)]
    wait_rows(parts, part_sems.at[1], regions - 1)
    mine = jnp.sum(parts[...], axis=0)
    part[...] = mine
    sums[me] = mine

    def to_peer(step):
        peer = (me + step) % peers
        pltpu.make_async_remote_copy(
            src_ref=part,
            dst_ref=sums.at[me],
            send_sem=sum_sems.at[0],
            recv_sem=sum_sems.at[1],
            device_id=(grp, peer),
            device_id_type=MESH,
        ).start()

    each(1, peers, to_peer)
    wait_rows(sums, sum_sems.at[1], peers - 1)
    whole[grp] = jnp.sum(sums[...], axis=0)
    over_regions(lambda other: whole.at[grp], whole, whole_sems)
    end_rims(halo)
    end_rims(echo)
    for half in range(2):
        for part_of in range(2):
            lanes = pl.ds(part_of * LANES, LANES)
            wait_blocks(outgoing.at[half], out_sems.at[half * 2 + part_of], lanes)
            wait_blocks(filled.at[half], filled_sems.at[half * 2 + part_of], lanes)
    wait_rows(parts, part_sems.at[0], regions - 1)
    wait_rows(sums, sum_sems.at[0], peers - 1)
    wait_rows(whole, whole_sems.at[0], regions - 1)
    wait_rows(whole, whole_sems.at[1], regions - 1)
    for k in range(TAPS):
        conv_ref[k : k + 1, :] = whole[k // share, k % share]


def hand_over(grad_ref, conv_ref, grad_out_ref, conv_out_ref):
    grad_out_ref[...] = grad_ref[...]
    conv_out_ref[...] = conv_ref[...]


def on_device(features, cotangent, conv_weight, neighbours, halo_index, send_index, curve_slot):
    peers, slots = send_index.shape[1:]
    regions = lax.axis_size("grp")
    flat = peers * slots
    share = -(-TAPS // regions)
    args = (
        neighbours.T,
        conv_weight,
        send_index.reshape(peers, slots),
        curve_slot.reshape(1, ROWS),
        halo_index,
        features,
        cotangent,
    )
    blocks = pltpu.VMEM((2, peers, slots, HALF), BF16)
    dma = pltpu.SemaphoreType.DMA
    results = pl.pallas_call(
        functools.partial(kernel, regions, peers, slots),
        out_shape=(
            jax.ShapeDtypeStruct((ROWS, D), BF16),
            jax.ShapeDtypeStruct((TAPS, D), F32),
        ),
        in_specs=[VMEM] * len(args),
        out_specs=(VMEM, VMEM),
        scratch_shapes=[
            pltpu.VMEM((TABLE, D), BF16),
            pltpu.VMEM((2 * RIM, D), BF16),
            pltpu.VMEM((flat, ROWS), BF16),
            pltpu.VMEM((ROWS, flat), BF16),
            pltpu.VMEM((ROWS, flat), BF16),
            pltpu.VMEM((flat, ROWS), BF16),
            pltpu.VMEM((2, ROWS, HALF), F32),
            blocks,
            blocks,
            pltpu.VMEM((ROWS, LANES), BF16),
            pltpu.VMEM((ROWS, LANES), BF16),
            blocks,
            blocks,
            pltpu.VMEM((ROWS, HALF), BF16),
            pltpu.VMEM((TABLE, HALF), F32),
            pltpu.VMEM((ROWS, D), F32),
            pltpu.VMEM((2 * RIM, D), BF16),
            pltpu.VMEM((2 * RIM, D), BF16),
            pltpu.VMEM((regions * share, 1, D), F32),
            pltpu.VMEM((regions, share, 1, D), F32),
            pltpu.VMEM((share, 1, D), F32),
            pltpu.VMEM((peers, share, 1, D), F32),
            pltpu.VMEM((regions, share, 1, D), F32),
            dma((4,)),
            dma((4,)),
            dma((4,)),
            dma((4,)),
            dma((4,)),
            dma((4,)),
            dma((2,)),
            dma((2,)),
            dma((2,)),
        ],
        compiler_params=pltpu.CompilerParams(
            vmem_limit_bytes=60 * 2**20, collective_id=0, has_side_effects=True
        ),
    )(*args)
    return pl.pallas_call(
        hand_over,
        out_shape=tuple(jax.ShapeDtypeStruct(a.shape, a.dtype) for a in results),
        in_specs=[VMEM, VMEM],
        out_specs=(VMEM, VMEM),
    )(*results)


def solution(mesh):
    in_specs = (
        P(("grp", "pt"), None),
        P(("grp", "pt"), None),
        P(),
        P(("grp", "pt"), None),
        P(("grp", "pt"), None),
        P(("grp", "pt"), None, None),
        P(("grp", "pt")),
    )
    out_specs = (P(("grp", "pt"), None), P())
    return jax.shard_map(
        on_device, mesh=mesh, in_specs=in_specs, out_specs=out_specs, check_vma=False
    )
```

time: 124 us -> 105 us (0.85)
  Pallas kernels: 120 us -> 104 us
  local copies, waits for them, and re-layouts: 3.92 us -> 0 us
    pallas_call x1, Pallas kernels: 120 us -> 102 us  [on_device(): pl.pallas_call(functools.partial(kernel, regions, peers, slots), out_shap...]
    unnamed x4 -> x0, local copies, waits for them, and re-layouts: 2.53 us -> none
    pallas_call x0 -> x1, Pallas kernels: none -> 1.88 us  [on_device(): pl.pallas_call(hand_over, out_shape=tuple((jax.ShapeDtypeStruct(a.shape,...]
    reshape x1 -> x0, local copies, waits for them, and re-layouts: 1.39 us -> none  [on_device(): send_index.reshape(1, flat)]
where the time goes in v3:
time: 105 us
  Pallas kernels  104 us (99%)
    pallas_call x1, Pallas kernels, on_device(): pl.pallas_call(functools.partial(kernel, regions, peers, slots), out_shap...  102 us

profile of v3, /device:TPU:1, one launch (start us, length us, event | category | flops | bytes accessed | tf_op | source)
XLA Modules:
  0.0 104.6 jit_solution(10911883475111171918)
XLA Ops:
  0.6 102.1 %shard_map.86 = (bf16[512,512]{1,0:T(8,128)(2,1)}, f32[27,512]{1,0:T(8,128)}) custom-call(s32[27,512]{1,0:T(8,128)} %bitcast.3, f32[27,512]{1,0:T(8,128)} %weight_ref.1, s32[32,32]{1,0:T(8,128)} %bitcast.4, s32[1,512]{1,0:T(1,128)} %bitcast.5, s32[1,128]{1,0:T(1,128)} %halo_ref.1, bf16[512,512]{1,0:T(8,128)(2,1)} %features_ref.1, bf16[512,512]{1,0:T(8,128)(2,1)} %cotangent_ref.1), custom_call_target="tpu_custom_call" | custom-call | tf_op jit(solution)/shard_map/pallas_call | solution.py:391
  102.7 1.9 %shard_map.87 = (bf16[512,512]{1,0:T(8,128)(2,1)}, f32[27,512]{1,0:T(8,128)}) custom-call(bf16[512,512]{1,0:T(8,128)(2,1)} %get-tuple-element.4.grad_ref, f32[27,512]{1,0:T(8,128)} %get-tuple-element.5.conv_ref), custom_call_target="tpu_custom_call" | custom-call | tf_op jit(solution)/shard_map/pallas_call | solution.py:437

commit v4 on v3

--- a/solution.py
+++ b/solution.py
@@ -109,6 +109,7 @@
     curve_rows,
     curve_columns,
     acc,
+    picks,
     outgoing,
     incoming,
     curve,
@@ -120,6 +121,7 @@
     total,
     rims,
     echoed,
+    partial,
     terms,
     parts,
     part,
@@ -198,13 +200,17 @@
         padded[ROWS + RIM :, :] = jnp.zeros((RIM, D), BF16)
         echoed[RIM:, :] = jnp.zeros((RIM, D), BF16)
 
-    def weighted(step, half, one_hot, table):
+    def weighted(step, half, one_hot, table, first):
         span = pl.ds(pl.multiple_of(half * HALF, HALF), HALF)
         added = jnp.zeros((ROWS, HALF), F32)
         for k in range(CENTRE):
             k = step * (CENTRE + 1) + k
             picked = dot(one_hot(taps_ref[pl.ds(k, 1), :]), table[:, span])
             added = added + picked * weight_ref[pl.ds(k, 1), span]
+            for part_of in range(2):
+                found = picked[:, part_of * LANES : (part_of + 1) * LANES].astype(BF16)
+                at = half * 2 + part_of
+                picks[at, k] = found if first else picks[at, k] + found
         return added
 
     def from_own(half):
@@ -213,11 +219,11 @@
         acc[half] = own + own * weight_ref[CENTRE : CENTRE + 1, span]
 
         def taps(step):
-            acc[half] += weighted(step, half, lambda row: rows_of(row, ROWS), padded.at[pl.ds(0, ROWS)])
+            acc[half] += weighted(step, half, lambda row: rows_of(row, ROWS), padded.at[pl.ds(0, ROWS)], True)
 
         each(0, 2, taps)
 
-    each(0, 2, from_own)
+    from_own(0)
     pl.semaphore_wait(barrier, peers - 1 + regions - 1)
     halo = rim_copies(lent, padded, halo_sems, ROWS + RIM, ROWS)
     start_rims(halo)
@@ -225,6 +231,7 @@
     send_columns[...] = columns_of(send_row, ROWS)
     curve_rows[...] = rows_of(curve_ref[...], flat)
     curve_columns[...] = columns_of(curve_ref[...], flat)
+    from_own(1)
     take_rims(halo)
 
     def send_block(source, target, send_sem, recv_sem, lanes):
@@ -249,7 +256,7 @@
     def forward(half):
         def taps(step):
             acc[half] += weighted(
-                step, half, lambda row: rows_of(row - ROWS, 2 * RIM), padded.at[pl.ds(ROWS, 2 * RIM)]
+                step, half, lambda row: rows_of(row - ROWS, 2 * RIM), padded.at[pl.ds(ROWS, 2 * RIM)], False
             )
 
         each(0, 2, taps)
@@ -279,35 +286,6 @@
 
     each(0, 4, attend)
 
-    def backward(half):
-        span = pl.ds(pl.multiple_of(half * HALF, HALF), HALF)
-        for part_of in range(2):
-            lanes = pl.ds(part_of * LANES, LANES)
-            wait_blocks(returned.at[half], returned_sems.at[half * 2 + part_of], lanes)
-        grad_hidden[...] = dot(send_columns[...], returned[half].reshape(flat, HALF)).astype(BF16)
-        grad = grad_hidden[...].astype(F32)
-        spread[:ROWS, :] = grad + grad * weight_ref[CENTRE : CENTRE + 1, span]
-        spread[ROWS:, :] = jnp.zeros((2 * RIM, HALF), F32)
-        terms[CENTRE, :, span] = jnp.sum(grad * padded[:ROWS, span].astype(F32), axis=0, keepdims=True)
-
-        def taps(step):
-            added = jnp.zeros((TABLE, HALF), F32)
-            for k in range(CENTRE):
-                k = step * (CENTRE + 1) + k
-                landed = dot(columns_of(taps_ref[pl.ds(k, 1), :], TABLE), grad_hidden[...])
-                terms[k, :, span] = jnp.sum(landed * padded[:, span].astype(F32), axis=0, keepdims=True)
-                added = added + landed * weight_ref[pl.ds(k, 1), span]
-            spread[...] += added
-
-        each(0, 2, taps)
-        total[:, span] = spread[:ROWS, :]
-        rims[:, span] = spread[ROWS:, :].astype(BF16)
-
-    each(0, 2, backward)
-
-    echo = rim_copies(rims, echoed, echo_sems, RIM, 0)
-    start_rims(echo)
-
     def over_regions(source, target, sems):
         def one(step):
             other = (grp + step) % regions
@@ -326,29 +304,78 @@
         view = buffer.at[pl.ds(0, count)]
         pltpu.make_async_copy(view, view, sem).wait()
 
-    over_regions(lambda other: terms.at[pl.ds(other * share, share)], parts, part_sems)
+    def scatter_terms():
+        over_regions(lambda other: terms.at[pl.ds(other * share, share)], parts, part_sems)
+
+    def exchange_parts():
+        parts[grp] = terms[pl.ds(grp * share, share)]
+        wait_rows(parts, part_sems.at[1], regions - 1)
+        mine = jnp.sum(parts[...], axis=0)
+        part[...] = mine
+        sums[me] = mine
+
+        def to_peer(step):
+            peer = (me + step) % peers
+            pltpu.make_async_remote_copy(
+                src_ref=part,
+                dst_ref=sums.at[me],
+                send_sem=sum_sems.at[0],
+                recv_sem=sum_sems.at[1],
+                device_id=(grp, peer),
+                device_id_type=MESH,
+            ).start()
+
+        each(1, peers, to_peer)
+
+    def backward(half):
+        span = pl.ds(pl.multiple_of(half * HALF, HALF), HALF)
+        for part_of in range(2):
+            lanes = pl.ds(part_of * LANES, LANES)
+            wait_blocks(returned.at[half], returned_sems.at[half * 2 + part_of], lanes)
+        grad_hidden[...] = dot(send_columns[...], returned[half].reshape(flat, HALF)).astype(BF16)
+        partial[...] = jnp.zeros((TAPS, 8, HALF), F32)
+
+        def sum_terms(block):
+            rows = pl.ds(pl.multiple_of(block * RIM, RIM), RIM)
+            for part_of in range(2):
+                lanes = slice(part_of * LANES, (part_of + 1) * LANES)
+                grad = grad_hidden[rows, lanes].astype(F32)
+                for k in range(TAPS):
+                    if k == CENTRE:
+                        found = padded[rows, span][:, lanes]
+                    else:
+                        found = picks[half * 2 + part_of, k, rows, :]
+                    product = (grad * found.astype(F32)).reshape(RIM // 8, 8, LANES)
+                    partial[k, :, lanes] += jnp.sum(product, axis=0)
+
+        each(0, ROWS // RIM, sum_terms)
+        terms[:TAPS, :, span] = jnp.sum(partial[...], axis=1, keepdims=True)
+        pl.when(half == 1)(scatter_terms)
+        grad = grad_hidden[...].astype(F32)
+        spread[:ROWS, :] = grad + grad * weight_ref[CENTRE : CENTRE + 1, span]
+        spread[ROWS:, :] = jnp.zeros((2 * RIM, HALF), F32)
+
+        def taps(step):
+            pl.when((half == 1) & (step == 1))(exchange_parts)
+            added = jnp.zeros((TABLE, HALF), F32)
+            for k in range(CENTRE):
+                k = step * (CENTRE + 1) + k
+                landed = dot(columns_of(taps_ref[pl.ds(k, 1), :], TABLE), grad_hidden[...])
+                added = added + landed * weight_ref[pl.ds(k, 1), span]
+            spread[...] += added
+
+        each(0, 2, taps)
+        total[:, span] = spread[:ROWS, :]
+        rims[:, span] = spread[ROWS:, :].astype(BF16)
+
+    each(0, 2, backward)
+
+    echo = rim_copies(rims, echoed, echo_sems, RIM, 0)
+    start_rims(echo)
 
     take_rims(echo)
     out_ref[...] = (total[...] + dot(columns_of(halo_ref[...], ROWS), echoed[...])).astype(BF16)
 
-    parts[grp] = terms[pl.ds(grp * share, share)]
-    wait_rows(parts, part_sems.at[1], regions - 1)
-    mine = jnp.sum(parts[...], axis=0)
-    part[...] = mine
-    sums[me] = mine
-
-    def to_peer(step):
-        peer = (me + step) % peers
-        pltpu.make_async_remote_copy(
-            src_ref=part,
-            dst_ref=sums.at[me],
-            send_sem=sum_sems.at[0],
-            recv_sem=sum_sems.at[1],
-            device_id=(grp, peer),
-            device_id_type=MESH,
-        ).start()
-
-    each(1, peers, to_peer)
     wait_rows(sums, sum_sems.at[1], peers - 1)
     whole[grp] = jnp.sum(sums[...], axis=0)
     over_regions(lambda other: whole.at[grp], whole, whole_sems)
@@ -404,6 +431,7 @@
             pltpu.VMEM((ROWS, flat), BF16),
             pltpu.VMEM((flat, ROWS), BF16),
             pltpu.VMEM((2, ROWS, HALF), F32),
+            pltpu.VMEM((4, TAPS, ROWS, LANES), BF16),
             blocks,
             blocks,
             pltpu.VMEM((ROWS, LANES), BF16),
@@ -415,6 +443,7 @@
             pltpu.VMEM((ROWS, D), F32),
             pltpu.VMEM((2 * RIM, D), BF16),
             pltpu.VMEM((2 * RIM, D), BF16),
+            pltpu.VMEM((TAPS, 8, HALF), F32),
             pltpu.VMEM((regions * share, 1, D), F32),
             pltpu.VMEM((regions, share, 1, D), F32),
             pltpu.VMEM((share, 1, D), F32),

time: 105 us -> 100 us (0.952)
  Pallas kernels: 104 us -> 99.2 us
    pallas_call x1, Pallas kernels: 102 us -> 97.3 us  [on_device(): pl.pallas_call(functools.partial(kernel, regions, peers, slots), out_shap...]
where the time goes in v4:
time: 100 us; the launch traced here: 99.8 us
  Pallas kernels  99.2 us (99%)
    pallas_call x1, Pallas kernels, on_device(): pl.pallas_call(functools.partial(kernel, regions, peers, slots), out_shap...  97.3 us

profile of v4, /device:TPU:1, one launch (start us, length us, event | category | flops | bytes accessed | tf_op | source)
XLA Modules:
  0.0 99.8 jit_solution(935899027260850545)
XLA Ops:
  0.6 97.3 %shard_map.86 = (bf16[512,512]{1,0:T(8,128)(2,1)}, f32[27,512]{1,0:T(8,128)}) custom-call(s32[27,512]{1,0:T(8,128)} %bitcast.3, f32[27,512]{1,0:T(8,128)} %weight_ref.1, s32[32,32]{1,0:T(8,128)} %bitcast.4, s32[1,512]{1,0:T(1,128)} %bitcast.5, s32[1,128]{1,0:T(1,128)} %halo_ref.1, bf16[512,512]{1,0:T(8,128)(2,1)} %features_ref.1, bf16[512,512]{1,0:T(8,128)(2,1)} %cotangent_ref.1), custom_call_target="tpu_custom_call" | custom-call | tf_op jit(solution)/shard_map/pallas_call | solution.py:418
  98.0 1.9 %shard_map.87 = (bf16[512,512]{1,0:T(8,128)(2,1)}, f32[27,512]{1,0:T(8,128)}) custom-call(bf16[512,512]{1,0:T(8,128)(2,1)} %get-tuple-element.4.grad_ref, f32[27,512]{1,0:T(8,128)} %get-tuple-element.5.conv_ref), custom_call_target="tpu_custom_call" | custom-call | tf_op jit(solution)/shard_map/pallas_call | solution.py:466

commit v5 on v4

--- a/solution.py
+++ b/solution.py
@@ -327,40 +327,50 @@
 
         each(1, peers, to_peer)
 
+    def finish_sums():
+        wait_rows(sums, sum_sems.at[1], peers - 1)
+        whole[grp] = jnp.sum(sums[...], axis=0)
+        over_regions(lambda other: whole.at[grp], whole, whole_sems)
+
+    def collect(index):
+        half = index // 2
+        lanes = pl.ds(pl.multiple_of(index % 2 * LANES, LANES), LANES)
+        span = pl.ds(pl.multiple_of(index * LANES, LANES), LANES)
+        wait_blocks(returned.at[half], returned_sems.at[index], lanes)
+        rows = returned[half, :, :, lanes].reshape(flat, LANES)
+        grad_hidden[:, span] = dot(send_columns[...], rows).astype(BF16)
+        partial[...] = jnp.zeros((TAPS, 8, LANES), F32)
+
+        def sum_terms(block):
+            rows = pl.ds(pl.multiple_of(block * RIM, RIM), RIM)
+            grad = grad_hidden[rows, span].astype(F32)
+            for k in range(TAPS):
+                found = padded[rows, span] if k == CENTRE else picks[index, k, rows, :]
+                product = (grad * found.astype(F32)).reshape(RIM // 8, 8, LANES)
+                partial[k] += jnp.sum(product, axis=0)
+
+        each(0, ROWS // RIM, sum_terms)
+        terms[:TAPS, :, span] = jnp.sum(partial[...], axis=1, keepdims=True)
+
+    def end_terms():
+        collect(3)
+        scatter_terms()
+
+    each(0, 3, collect)
+
     def backward(half):
         span = pl.ds(pl.multiple_of(half * HALF, HALF), HALF)
-        for part_of in range(2):
-            lanes = pl.ds(part_of * LANES, LANES)
-            wait_blocks(returned.at[half], returned_sems.at[half * 2 + part_of], lanes)
-        grad_hidden[...] = dot(send_columns[...], returned[half].reshape(flat, HALF)).astype(BF16)
-        partial[...] = jnp.zeros((TAPS, 8, HALF), F32)
-
-        def sum_terms(block):
-            rows = pl.ds(pl.multiple_of(block * RIM, RIM), RIM)
-            for part_of in range(2):
-                lanes = slice(part_of * LANES, (part_of + 1) * LANES)
-                grad = grad_hidden[rows, lanes].astype(F32)
-                for k in range(TAPS):
-                    if k == CENTRE:
-                        found = padded[rows, span][:, lanes]
-                    else:
-                        found = picks[half * 2 + part_of, k, rows, :]
-                    product = (grad * found.astype(F32)).reshape(RIM // 8, 8, LANES)
-                    partial[k, :, lanes] += jnp.sum(product, axis=0)
-
-        each(0, ROWS // RIM, sum_terms)
-        terms[:TAPS, :, span] = jnp.sum(partial[...], axis=1, keepdims=True)
-        pl.when(half == 1)(scatter_terms)
-        grad = grad_hidden[...].astype(F32)
+        grad = grad_hidden[:, span].astype(F32)
         spread[:ROWS, :] = grad + grad * weight_ref[CENTRE : CENTRE + 1, span]
         spread[ROWS:, :] = jnp.zeros((2 * RIM, HALF), F32)
 
         def taps(step):
-            pl.when((half == 1) & (step == 1))(exchange_parts)
+            pl.when((half == 0) & (step == 1))(end_terms)
+            pl.when((half == 1) & (step == 0))(exchange_parts)
             added = jnp.zeros((TABLE, HALF), F32)
             for k in range(CENTRE):
                 k = step * (CENTRE + 1) + k
-                landed = dot(columns_of(taps_ref[pl.ds(k, 1), :], TABLE), grad_hidden[...])
+                landed = dot(columns_of(taps_ref[pl.ds(k, 1), :], TABLE), grad_hidden[:, span])
                 added = added + landed * weight_ref[pl.ds(k, 1), span]
             spread[...] += added
 
@@ -372,13 +382,10 @@
 
     echo = rim_copies(rims, echoed, echo_sems, RIM, 0)
     start_rims(echo)
-
+    finish_sums()
     take_rims(echo)
     out_ref[...] = (total[...] + dot(columns_of(halo_ref[...], ROWS), echoed[...])).astype(BF16)
 
-    wait_rows(sums, sum_sems.at[1], peers - 1)
-    whole[grp] = jnp.sum(sums[...], axis=0)
-    over_regions(lambda other: whole.at[grp], whole, whole_sems)
     end_rims(halo)
     end_rims(echo)
     for half in range(2):
@@ -438,12 +445,12 @@
             pltpu.VMEM((ROWS, LANES), BF16),
             blocks,
             blocks,
-            pltpu.VMEM((ROWS, HALF), BF16),
+            pltpu.VMEM((ROWS, D), BF16),
             pltpu.VMEM((TABLE, HALF), F32),
             pltpu.VMEM((ROWS, D), F32),
             pltpu.VMEM((2 * RIM, D), BF16),
             pltpu.VMEM((2 * RIM, D), BF16),
-            pltpu.VMEM((TAPS, 8, HALF), F32),
+            pltpu.VMEM((TAPS, 8, LANES), F32),
             pltpu.VMEM((regions * share, 1, D), F32),
             pltpu.VMEM((regions, share, 1, D), F32),
             pltpu.VMEM((share, 1, D), F32),

time: 100 us -> 99.2 us (level)
  no operation moved by 1% of the time
where the time goes in v5:
time: 99.2 us; the launch traced here: 99 us
  Pallas kernels  98.4 us (99%)
    pallas_call x1, Pallas kernels, on_device(): pl.pallas_call(functools.partial(kernel, regions, peers, slots), out_shap...  96.5 us

profile of v5, /device:TPU:1, one launch (start us, length us, event | category | flops | bytes accessed | tf_op | source)
XLA Modules:
  0.0 99.0 jit_solution(10201269518538768744)
XLA Ops:
  0.6 96.5 %shard_map.86 = (bf16[512,512]{1,0:T(8,128)(2,1)}, f32[27,512]{1,0:T(8,128)}) custom-call(s32[27,512]{1,0:T(8,128)} %bitcast.3, f32[27,512]{1,0:T(8,128)} %weight_ref.1, s32[32,32]{1,0:T(8,128)} %bitcast.4, s32[1,512]{1,0:T(1,128)} %bitcast.5, s32[1,128]{1,0:T(1,128)} %halo_ref.1, bf16[512,512]{1,0:T(8,128)(2,1)} %features_ref.1, bf16[512,512]{1,0:T(8,128)(2,1)} %cotangent_ref.1), custom_call_target="tpu_custom_call" | custom-call | tf_op jit(solution)/shard_map/pallas_call | solution.py:425
  97.1 1.9 %shard_map.87 = (bf16[512,512]{1,0:T(8,128)(2,1)}, f32[27,512]{1,0:T(8,128)}) custom-call(bf16[512,512]{1,0:T(8,128)(2,1)} %get-tuple-element.4.grad_ref, f32[27,512]{1,0:T(8,128)} %get-tuple-element.5.conv_ref), custom_call_target="tpu_custom_call" | custom-call | tf_op jit(solution)/shard_map/pallas_call | solution.py:473

commit v6 on v5

--- a/solution.py
+++ b/solution.py
@@ -473,8 +473,15 @@
     return pl.pallas_call(
         hand_over,
         out_shape=tuple(jax.ShapeDtypeStruct(a.shape, a.dtype) for a in results),
-        in_specs=[VMEM, VMEM],
-        out_specs=(VMEM, VMEM),
+        grid=(4,),
+        in_specs=[
+            pl.BlockSpec((ROWS // 4, D), lambda i: (i, 0)),
+            pl.BlockSpec((TAPS, D), lambda i: (0, 0)),
+        ],
+        out_specs=(
+            pl.BlockSpec((ROWS // 4, D), lambda i: (i, 0)),
+            pl.BlockSpec((TAPS, D), lambda i: (0, 0)),
+        ),
     )(*results)
 
 

time: 99.2 us -> 100 us (level)
  Pallas kernels: 98.4 us -> 99.7 us
    pallas_call x1, Pallas kernels: 1.88 us -> 3.18 us  [on_device(): pl.pallas_call(hand_over, out_shape=tuple((jax.ShapeDtypeStruct(a.shape,...]
where the time goes in v6:
time: 100 us
  Pallas kernels  99.7 us (100%)
    pallas_call x1, Pallas kernels, on_device(): pl.pallas_call(functools.partial(kernel, regions, peers, slots), out_shap...  96.5 us
    pallas_call x1, Pallas kernels, on_device(): pl.pallas_call(hand_over, out_shape=tuple((jax.ShapeDtypeStruct(a.shape,...  3.18 us

profile of v6, /device:TPU:1, one launch (start us, length us, event | category | flops | bytes accessed | tf_op | source)
XLA Modules:
  0.0 100.3 jit_solution(6698111672915605888)
XLA Ops:
  0.6 96.5 %shard_map.86 = (bf16[512,512]{1,0:T(8,128)(2,1)}, f32[27,512]{1,0:T(8,128)}) custom-call(s32[27,512]{1,0:T(8,128)} %bitcast.3, f32[27,512]{1,0:T(8,128)} %weight_ref.1, s32[32,32]{1,0:T(8,128)} %bitcast.4, s32[1,512]{1,0:T(1,128)} %bitcast.5, s32[1,128]{1,0:T(1,128)} %halo_ref.1, bf16[512,512]{1,0:T(8,128)(2,1)} %features_ref.1, bf16[512,512]{1,0:T(8,128)(2,1)} %cotangent_ref.1), custom_call_target="tpu_custom_call" | custom-call | tf_op jit(solution)/shard_map/pallas_call | solution.py:425
  97.1 3.2 %shard_map.87 = (bf16[512,512]{1,0:T(8,128)(2,1)}, f32[27,512]{1,0:T(8,128)}) custom-call(bf16[512,512]{1,0:T(8,128)(2,1)} %get-tuple-element.4.grad_ref, f32[27,512]{1,0:T(8,128)} %get-tuple-element.5.conv_ref), custom_call_target="tpu_custom_call" | custom-call | tf_op jit(solution)/shard_map/pallas_call | solution.py:473
